TPU v7x, 128 devices: a whole 4x4x4 slice. The times are simulated.
128 devices in a mesh: seq: 16 (over x, y), dp: 8 (over z, core).
Axes of the slice: x: 4, y: 4, z: 4, core: 2. Of those that a mesh axis runs over, the one named last changes fastest.
Arguments:
- inputs: bfloat16 [8, 4096, 2048], P('dp', 'seq'), may hold values from -32 to 32
- w_qkv: bfloat16 [2048, 3072], replicated, may hold values from -0.088388348 to 0.088388348
- random_blocks: int32 [32, 3], replicated, may hold values from 0 to 31, as said below
- d_out: bfloat16 [8, 4096, 2048], P('dp', 'seq'), may hold values from -6 to 6
Outputs:
- attended: bfloat16 [8, 4096, 2048], P('dp', 'seq')
- d_wqkv: float32 [2048, 3072], P(('seq', 'dp'))
Inputs may be any that keep to these rules, and one draw needn't show every extreme that they name: `random_blocks`: for each j, the 6 entries of rows j * 2 to (j + 1) * 2 - 1 lie in different groups of 2 consecutive blocks (entry // 2), none of them group j.
All inputs are finite; a program needn't handle non-finite values.
Results may differ from a plain program's by a relative error of at most 0.02.
Values may be sent and summed in bfloat16 or wider, within the bound.
A program may use at most 192 MiB of HBM per device.

v0:
```python
import jax
import jax.numpy as jnp
from jax import lax
from jax.sharding import PartitionSpec as P

H = 16
KVH = 4
HD = 128
BLOCK = 128
NRAND = 3


def padded(array, sides, width):
    for axis, dim in sides:
        devices, length = (lax.axis_size(axis), array.shape[dim])
        up = [(i, (i + 1) % devices) for i in range(devices)]
        down = [(j, i) for i, j in up]
        last = lax.slice_in_dim(array, length - width, length, axis=dim)
        first = lax.slice_in_dim(array, 0, width, axis=dim)
        before = lax.ppermute(last, axis, up)
        after = lax.ppermute(first, axis, down)
        array = jnp.concatenate([before, array, after], axis=dim)
    return array


def broadcast(value, axis, source):
    kept = jnp.where(lax.axis_index(axis) == source, value, 0).astype(value.dtype)
    return lax.psum(kept, axis)


def from_behind(value, axis, steps):
    count = lax.axis_size(axis)
    pairs = [(source, (source + steps) % count) for source in range(count)]
    return lax.ppermute(value, axis, pairs)


def attend(q_block, key_tiles, dout_block):
    group = H // KVH
    scale = HD ** (-0.5)
    queries = q_block.reshape(BLOCK, KVH, group, HD)
    keys = key_tiles[:, : KVH * HD].reshape(-1, KVH, HD)
    values = key_tiles[:, KVH * HD :].reshape(-1, KVH, HD)
    scores = jnp.einsum("qgrd,kgd->grqk", queries, keys, preferred_element_type=jnp.float32) * scale
    peak = jnp.max(scores, axis=-1, keepdims=True)
    expos = jnp.exp(scores - peak)
    probs = expos / jnp.sum(expos, axis=-1, keepdims=True)
    weights = probs.astype(jnp.bfloat16)
    attended = jnp.einsum("grqk,kgd->qgrd", weights, values, preferred_element_type=jnp.float32)
    attended = attended.reshape(BLOCK, H * HD).astype(jnp.bfloat16)
    grads = dout_block.reshape(BLOCK, KVH, group, HD)
    dprob = jnp.einsum("qgrd,kgd->grqk", grads, values, preferred_element_type=jnp.float32)
    dscore = probs * (dprob - jnp.sum(probs * dprob, axis=-1, keepdims=True))
    dweights = (dscore * scale).astype(jnp.bfloat16)
    d_query = jnp.einsum("grqk,kgd->qgrd", dweights, keys, preferred_element_type=jnp.float32)
    d_query = d_query.reshape(BLOCK, H * HD).astype(jnp.bfloat16)
    d_key = jnp.einsum("grqk,qgrd->kgd", dweights, queries, preferred_element_type=jnp.float32)
    d_value = jnp.einsum("grqk,qgrd->kgd", weights, grads, preferred_element_type=jnp.float32)
    terms = jnp.concatenate([d_key.reshape(-1, KVH * HD), d_value.reshape(-1, KVH * HD)], axis=-1)
    return (attended, d_query, terms)


def attend_triple(triple):
    return attend(triple[0], triple[1], triple[2])


def body(inputs, w_qkv, random_blocks, d_out):
    seq_dev, tok, width = inputs.shape
    n_seq = lax.axis_size("seq")
    position = lax.axis_index("seq")
    per_device = tok // BLOCK
    kv_width = 2 * KVH * HD
    q_width = H * HD
    flat_in = inputs.reshape(-1, width)
    projected = jnp.dot(flat_in, w_qkv, preferred_element_type=jnp.float32).astype(jnp.bfloat16)
    projected = projected.reshape(seq_dev, tok, -1)
    queries = projected[:, :, :q_width]
    kv_local = projected[:, :, q_width:]
    extended = padded(kv_local, (("seq", 1),), BLOCK)
    extended = extended.reshape(seq_dev, per_device + 2, BLOCK, kv_width)
    window_index = jnp.arange(per_device)[:, None] + jnp.arange(3)[None, :]
    window = extended[:, window_index]
    global_kv = broadcast(kv_local, "seq", 0)
    global_kv = jnp.broadcast_to(
        global_kv.reshape(seq_dev, 1, 2, BLOCK, kv_width), (seq_dev, per_device, 2, BLOCK, kv_width)
    )
    my_random = lax.dynamic_slice_in_dim(
        random_blocks, position * per_device, per_device, 0
    ).reshape(-1)
    empty_tiles = jnp.zeros((seq_dev, my_random.shape[0], BLOCK, kv_width), jnp.bfloat16)
    piece = lax.all_gather(kv_local, "seq", axis=1, tiled=True)
    rows = piece.shape[1]
    wanted = my_random[:, None] * BLOCK + jnp.arange(BLOCK)[None, :]
    inside = (wanted >= 0) & (wanted < rows)
    taken = jnp.take(piece, jnp.clip(wanted, 0, rows - 1).reshape(-1), axis=1).reshape(
        empty_tiles.shape
    )
    far_tiles = jnp.where(inside[None, :, :, None], taken, empty_tiles)
    far_tiles = far_tiles.reshape(seq_dev, per_device, NRAND, BLOCK, kv_width)
    picked = jnp.concatenate([window, global_kv, far_tiles], axis=2)
    listed = picked.shape[2]
    picked = picked.reshape(seq_dev * per_device, listed * BLOCK, kv_width)
    query_blocks = queries.reshape(seq_dev * per_device, BLOCK, q_width)
    grad_blocks = d_out.reshape(seq_dev * per_device, BLOCK, q_width)
    attended, d_query, terms = lax.map(attend_triple, (query_blocks, picked, grad_blocks))
    terms = terms.reshape(seq_dev, per_device, listed, BLOCK, kv_width)
    rim_sums = jnp.zeros((seq_dev, per_device + 2, BLOCK, kv_width), jnp.float32)
    rim_sums = rim_sums.at[:, window_index].add(terms[:, :, :3])
    from_next = from_behind(rim_sums[:, 0].astype(jnp.bfloat16), "seq", -1).astype(jnp.float32)
    from_prev = from_behind(rim_sums[:, -1].astype(jnp.bfloat16), "seq", 1).astype(jnp.float32)
    summed = rim_sums[:, 1:-1]
    summed = summed.at[:, -1].add(from_next).at[:, 0].add(from_prev)
    global_sum = lax.psum(jnp.sum(terms[:, :, 3:5], axis=1).astype(jnp.bfloat16), "seq").astype(
        jnp.float32
    )
    summed = summed.at[:, :2].add(jnp.where(position == 0, global_sum, 0.0))
    far_terms = terms[:, :, 5:].reshape(seq_dev, -1, BLOCK, kv_width)
    spread = jnp.zeros((seq_dev, n_seq * per_device, BLOCK, kv_width), jnp.float32)
    spread = spread.at[:, my_random].add(far_terms)
    summed = summed + lax.psum_scatter(
        spread.astype(jnp.bfloat16), "seq", scatter_dimension=1, tiled=True
    ).astype(jnp.float32)
    d_kv = summed.astype(jnp.bfloat16).reshape(seq_dev, tok, kv_width)
    d_qkv = jnp.concatenate([d_query.reshape(seq_dev, tok, q_width), d_kv], axis=-1).reshape(
        seq_dev * tok, -1
    )
    section = lax.psum_scatter(
        lax.dot_general(
            flat_in, d_qkv, (((0,), (0,)), ((), ())), preferred_element_type=jnp.float32
        ).astype(jnp.bfloat16),
        "seq",
        scatter_dimension=0,
        tiled=True,
    )
    d_wqkv = lax.psum_scatter(section, "dp", scatter_dimension=0, tiled=True).astype(jnp.float32)
    return (attended.reshape(seq_dev, tok, q_width), d_wqkv)


def solution(mesh):
    return jax.shard_map(
        body,
        mesh=mesh,
        in_specs=(P("dp", "seq", None), P(), P(), P("dp", "seq", None)),
        out_specs=(P("dp", "seq", None), P(("seq", "dp"), None)),
        check_vma=False,
    )
```

profile of v0, /device:TPU:1, one launch (start us, length us, event | category | flops | bytes accessed | tf_op | source)
XLA Modules:
  0.0 675.7 jit_solution(6592958365345150991)
XLA Ops:
  7.2 1.2 copy-done
  8.4 8.0 %fusion.29 = bf16[1,256,3072]{2,1,0:T(8,128)(2,1)S(1)} fusion(bf16[2048,3072]{1,0:T(8,128)(2,1)} %param.15, bf16[1,256,2048]{2,1,0:T(8,128)(2,1)S(1)} %copy-done), kind=kOutput, calls=%fused_computation.44 | convolution fusion | flops 3222011904 | bytes 15204352 | tf_op jit(solution)/shard_map/dot_general | solution.py:74
  16.4 1.1 broadcast_select_fusion
  18.3 2.1 collective-permute-start
  20.4 3.6 collective-permute-start.1
  25.5 4.9 collective-permute-done
  30.4 2.1 pad_maximum_fusion.1
  32.5 3.1 gather_fusion
  35.6 55.9 %all-gather.2.cloned.1.call-done = bf16[1,4096,1024]{2,1,0:T(8,128)(2,1)} async-done(((bf16[1,256,1024]{2,1,0:T(8,128)(2,1)}), bf16[1,4096,1024]{2,1,0:T(8,128)(2,1)}) %all-gather.2.cloned.1.call-update) | async-done | bytes 8388624 | tf_op jit(solution)/shard_map/all_gather | solution.py:90
  91.5 8.3 %gather_fusion.1 = bf16[768,1024]{1,0:T(8,128)(2,1)S(1)} fusion(bf16[4096,1024]{1,0:T(8,128)(2,1)} %bitcast.200, s32[1024]{0:T(1024)S(1)} %pad_clamp_fusion), kind=kCustom, calls=%fused_computation.1 | custom fusion | bytes 3148800 | tf_op jit(solution)/shard_map/jit(_take)/gather | solution.py:94
  99.8 1.5 select_select_fusion
  101.3 76.8 %all-reduce.3.cloned.1.call-done = bf16[2,128,1024]{2,1,0:T(8,128)(2,1)} async-done(((bf16[2,128,1024]{2,1,0:T(8,128)(2,1)}), bf16[2,128,1024]{2,1,0:T(8,128)(2,1)}) %all-reduce.3.cloned.1.call-update) | async-done | bytes 524304 | tf_op jit(solution)/shard_map/psum | solution.py:28
  178.1 1.2 broadcast_in_dim.65
  179.3 3.7 pad_maximum_fusion
  182.9 150.4 %while.18 = (s32[]{:T(128)}, bf16[2,128,2048]{2,1,0:T(8,128)(2,1)}, bf16[2,128,2048]{2,1,0:T(8,128)(2,1)}, f32[2,1024,1024]{2,1,0:T(8,128)}, bf16[2,1024,1024]{2...) while((s32[]{:T(128)}, bf16[2,128,2048]{2,1,0:T(8,128)(2,1)}, ...), condition=%wide.region_5.6_spmd, body=%wide.region_1.0_spmd.sunk | while | flops 3266845696 | bytes 164667824 | solution.py:104
  182.9 1.5 constant_dynamic-slice_fusion.9
  186.5 3.1 constant_dynamic-slice_fusion.8
  189.6 2.9 copy.112
  192.5 1.2 fusion.85
  193.6 1.1 copy-done.1
  194.7 4.5 fusion.86
  199.2 7.4 %fusion.87 = (f32[4,4,128]{2,1,0:T(4,128)S(1)}, f32[4,4,128,1024]{2,3,1,0:T(8,128)}) fusion(bf16[1024,4,128,1]{0,2,3,1:T(8,128)(2,1)S(1)} %bitcast.198, bf16[128,4,4,128]{0,3,2,1:T(8,128)(2,1)} %bitcast.201), kind=kOutput, calls=%fused_computation.81.clone.1 | convolution fusion | flops 543163392 | bytes 9969664 | tf_op jit(solution)/shard_map/while/body/eval_jaxpr/sub | solution.py:45
  206.6 5.0 fusion.89
  211.6 13.8 %fusion.88 = bf16[4,128,4,128]{3,1,2,0:T(8,128)(2,1)} fusion(bf16[1024,4,128,1]{0,2,3,1:T(8,128)(2,1)S(1)} %bitcast.199, f32[4,1024,128,4]{2,1,3,0:T(8,128)} %fusion.86, f32[4,4,128,1024]{2,3,1,0:T(8,128)} %get-tuple-element.200, f32[4,4,128]{2,1,0:T(4,128)S(1)} %get-tuple-element.201), kind=kOutput, calls=%fused_computation.27.clone.1 | convolution fusion | flops 551816192 | bytes 18358272 | tf_op jit(solution)/shard_map/while/body/eval_jaxpr/grqk,kgd->qgrd/dot_general | solution.py:54
  225.3 13.5 %fusion.91 = f32[4,128,1024,1]{2,1,3,0:T(8,128)} fusion(bf16[128,4,4,128]{0,3,2,1:T(8,128)(2,1)S(1)} %bitcast.202, f32[4,1024,128,4]{2,1,3,0:T(8,128)} %fusion.86, f32[4,4,128,1024]{2,3,1,0:T(8,128)} %get-tuple-element.200, f32[4,4,128]{2,1,0:T(4,128)S(1)} %get-tuple-element.201), kind=kOutput, calls=%fused_computation.20.clone.1 | convolution fusion | flops 551554048 | bytes 19406848 | tf_op jit(solution)/shard_map/while/body/eval_jaxpr/grqk,qgrd->kgd/dot_general | solution.py:56
  238.9 5.0 fusion.90
  243.9 2.5 maximum_bitcast_fusion.4
  246.4 5.5 copy.117
  252.3 1.0 constant_dynamic-update-slice_fusion.5
  253.3 4.8 constant_dynamic-update-slice_fusion.6
  258.2 1.4 constant_dynamic-slice_fusion.9
  261.7 3.1 constant_dynamic-slice_fusion.8
  264.8 2.9 copy.112
  267.7 1.2 fusion.85
  268.8 1.1 copy-done.1
  269.9 4.5 fusion.86
  274.4 7.4 %fusion.87 = (f32[4,4,128]{2,1,0:T(4,128)S(1)}, f32[4,4,128,1024]{2,3,1,0:T(8,128)}) fusion(bf16[1024,4,128,1]{0,2,3,1:T(8,128)(2,1)S(1)} %bitcast.198, bf16[128,4,4,128]{0,3,2,1:T(8,128)(2,1)} %bitcast.201), kind=kOutput, calls=%fused_computation.81.clone.1 | convolution fusion | flops 543163392 | bytes 9969664 | tf_op jit(solution)/shard_map/while/body/eval_jaxpr/sub | solution.py:45
  281.8 5.0 fusion.89
  286.8 13.8 %fusion.88 = bf16[4,128,4,128]{3,1,2,0:T(8,128)(2,1)} fusion(bf16[1024,4,128,1]{0,2,3,1:T(8,128)(2,1)S(1)} %bitcast.199, f32[4,1024,128,4]{2,1,3,0:T(8,128)} %fusion.86, f32[4,4,128,1024]{2,3,1,0:T(8,128)} %get-tuple-element.200, f32[4,4,128]{2,1,0:T(4,128)S(1)} %get-tuple-element.201), kind=kOutput, calls=%fused_computation.27.clone.1 | convolution fusion | flops 551816192 | bytes 18358272 | tf_op jit(solution)/shard_map/while/body/eval_jaxpr/grqk,kgd->qgrd/dot_general | solution.py:54
  300.5 13.5 %fusion.91 = f32[4,128,1024,1]{2,1,3,0:T(8,128)} fusion(bf16[128,4,4,128]{0,3,2,1:T(8,128)(2,1)S(1)} %bitcast.202, f32[4,1024,128,4]{2,1,3,0:T(8,128)} %fusion.86, f32[4,4,128,1024]{2,3,1,0:T(8,128)} %get-tuple-element.200, f32[4,4,128]{2,1,0:T(4,128)S(1)} %get-tuple-element.201), kind=kOutput, calls=%fused_computation.20.clone.1 | convolution fusion | flops 551554048 | bytes 19406848 | tf_op jit(solution)/shard_map/while/body/eval_jaxpr/grqk,qgrd->kgd/dot_general | solution.py:56
  314.1 5.0 fusion.90
  319.1 2.5 maximum_bitcast_fusion.4
  321.6 5.5 copy.117
  327.5 1.0 constant_dynamic-update-slice_fusion.5
  328.5 4.8 constant_dynamic-update-slice_fusion.6
  333.4 2.7 slice_reduce_fusion
  336.1 6.6 fusion.44
  342.7 7.9 %broadcast.277 = f32[32,128,1024]{2,1,0:T(8,128)} broadcast(f32[]{:T(128)} %constant.145.clone.1), dimensions={} | broadcast | bytes 16777220 | tf_op jit(solution)/shard_map/broadcast_in_dim | solution.py:117
  350.6 8.8 %scatter_fusion.1 = f32[32,128,1024]{2,1,0:T(8,128)} fusion(f32[32,128,1024]{2,1,0:T(8,128)} %broadcast.277, s32[6]{0:T(128)S(1)} %copy-done.17, f32[6,128,1024]{2,1,0:T(8,128)} %bitcast.207), kind=kCustom, calls=%fused_computation.3 | custom fusion | flops 786432 | bytes 9437208 | tf_op jit(solution)/shard_map/scatter-add | solution.py:118
  359.4 9.1 %convert_bitcast_fusion.1 = bf16[1,32,128,1024]{3,2,1,0:T(8,128)(2,1)} fusion(f32[32,128,1024]{2,1,0:T(8,128)} %scatter_fusion.1), kind=kLoop, calls=%fused_computation.41 | loop fusion | flops 4194304 | bytes 25165824 | tf_op jit(solution)/shard_map/convert_element_type | solution.py:120
  369.2 5.3 scatter_fusion
  374.7 2.4 collective-permute-start.2
  377.1 1.1 slice.142
  378.3 2.7 collective-permute-done.2
  381.9 3.9 collective-permute-done.3
  385.8 1.9 fusion.34
  387.7 39.7 %all-reduce.5.cloned.1.call-done = bf16[1,2,128,1024]{3,2,1,0:T(8,128)(2,1)} async-done(((bf16[1,2,128,1024]{3,2,1,0:T(8,128)(2,1)}), bf16[1,2,128,1024]{3,2,1,0:T(8,128)(2,1)}) %all-reduce.5.cloned.1.call-update) | async-done | bytes 524304 | tf_op jit(solution)/shard_map/psum | solution.py:112
  427.4 88.0 %reduce-scatter.8.cloned.1.call-done = bf16[1,2,128,1024]{3,2,1,0:T(8,128)(2,1)} async-done(((bf16[1,32,128,1024]{3,2,1,0:T(8,128)(2,1)}), bf16[1,2,128,1024]{3,2,1,0:T(8,128)(2,1)}) %reduce-scatter.8.cloned.1.call-update) | async-done | bytes 524304 | tf_op jit(solution)/shard_map/reduce_scatter | solution.py:119
  515.4 1.7 add_convert_fusion
  517.1 7.6 %convert_bitcast_fusion = bf16[2048,3072]{0,1:T(8,128)(2,1)} fusion(bf16[1,256,1024]{2,1,0:T(8,128)(2,1)S(1)} %bitcast.216, bf16[1,256,2048]{2,1,0:T(8,128)(2,1)} %bitcast.217, bf16[1,256,2048]{2,1,0:T(8,128)(2,1)S(1)} %copy-done), kind=kOutput, calls=%fused_computation.40 | convolution fusion | flops 3230662656 | bytes 15204352 | tf_op jit(solution)/shard_map/dot_general | solution.py:127
  524.8 16.7 %copy.90 = bf16[2048,3072]{1,0:T(8,128)(2,1)} copy(bf16[2048,3072]{0,1:T(8,128)(2,1)} %convert_bitcast_fusion) | data formatting | bytes 25165824
  541.5 94.8 %reduce-scatter.10.cloned.1.call-done = bf16[128,3072]{1,0:T(8,128)(2,1)} async-done(((bf16[2048,3072]{1,0:T(8,128)(2,1)}), bf16[128,3072]{1,0:T(8,128)(2,1)}) %reduce-scatter.10.cloned.1.call-update) | async-done | bytes 786448
  636.3 30.3 %reduce-scatter.12.cloned.1.call-done = bf16[16,3072]{1,0:T(8,128)(2,1)} async-done(((bf16[128,3072]{1,0:T(8,128)(2,1)}), bf16[16,3072]{1,0:T(8,128)(2,1)}) %reduce-scatter.12.cloned.1.call-update) | async-done | bytes 98320
  666.6 1.3 copy.93
  (103 shorter events, 10.1 us)
Async XLA Ops:
  7.2 1.2 copy-start
  7.2 84.3 %all-gather.2.cloned.1.call-start = ((), (), s32[]{:S(2)}) async-start(), calls=%async_computation.4 | async-start | bytes 8912896 | tf_op jit(solution)/shard_map/all_gather | solution.py:90
  8.4 15.8 %copy-start.16 = (s32[32,3]{0,1:T(4,128)S(1)}, s32[32,3]{0,1:T(4,128)}, u32[]{:S(2)}) copy-start(s32[32,3]{0,1:T(4,128)} %param.16) | copy-start | bytes 1156
  16.4 19.2 %copy-start.10 = (bf16[1,256,3072]{2,1,0:T(8,128)(2,1)}, bf16[1,256,3072]{2,1,0:T(8,128)(2,1)S(1)}, u32[]{:S(2)}) copy-start(bf16[1,256,3072]{2,1,0:T(8,128)(2,1)S(1)} %fusion.29) | copy-start | bytes 4718596
  17.5 12.9 %copy-start.13 = (bf16[1,256,1024]{2,1,0:T(8,128)(2,1)S(1)}, bf16[1,256,1024]{2,1,0:T(8,128)(2,1)}, u32[]{:S(2)}) copy-start(bf16[1,256,1024]{2,1,0:T(8,128)(2,1)} %get-tuple-element.144) | copy-start | bytes 1572868
  17.5 160.5 %all-reduce.3.cloned.1.call-start = ((), (), s32[]{:S(2)}) async-start(), calls=%async_computation.3 | async-start | bytes 1048576 | tf_op jit(solution)/shard_map/psum | solution.py:28
  18.3 12.0 %collective-permute-start = (bf16[1,128,1024]{2,1,0:T(8,128)(2,1)}, bf16[1,128,1024]{2,1,0:T(8,128)(2,1)}, u32[]{:S(2)}, u32[]{:S(2)}) collective-permute-start(bf16[1,128,1024]{2,1,0:T(8,128)(2,1)} %get-tuple-element.141), channel_id=1, source_target_pairs={{0,8},{8,16},{16,24},{24,32},{32,40},{40,48},{48,56},{56,64},{64,7... | collective-permute-start | bytes 786440 | tf_op jit(solution)/shard_map/ppermute | solution.py:20
  20.4 9.9 %collective-permute-start.1 = (bf16[1,128,1024]{2,1,0:T(8,128)(2,1)S(1)}, bf16[1,128,1024]{2,1,0:T(8,128)(2,1)}, u32[]{:S(2)}, u32[]{:S(2)}) collective-permute-start(bf16[1,128,1024]{2,1,0:T(8,128)(2,1)S(1)} %get-tuple-element.142), channel_id=1, source_target_pairs={{8,0},{16,8},{24,16},{32,24},{40,32},{48,40},{56,48},{64,56},{72,6... | collective-permute-start | bytes 786440 | tf_op jit(solution)/shard_map/ppermute | solution.py:21
  24.1 403.3 %all-reduce.5.cloned.1.call-start = ((), (), s32[]{:S(2)}) async-start(), calls=%async_computation.5 | async-start | bytes 1048576 | tf_op jit(solution)/shard_map/psum | solution.py:112
  25.5 74.3 %copy-start.14 = (s32[6]{0:T(128)}, s32[6]{0:T(128)S(1)}, u32[]{:S(2)}) copy-start(s32[6]{0:T(128)S(1)} %reshape.430) | copy-start | bytes 76
  179.3 3.7 slice-start
  182.9 3.6 copy-start.11
  192.5 2.2 copy-start.3
  193.6 1.1 copy-start.1
  194.7 4.5 copy-start.6
  199.2 7.4 %copy-start.2 = (bf16[1024,512]{0,1:T(8,128)(2,1)S(1)}, bf16[1024,512]{0,1:T(8,128)(2,1)}, u32[]{:S(2)}) copy-start(bf16[1024,512]{0,1:T(8,128)(2,1)} %copy-done.1) | copy-start | bytes 3145732 | tf_op jit(solution)/shard_map/while
  211.6 13.8 %copy-start.7 = (bf16[1,128,2048]{1,2,0:T(8,128)(2,1)S(1)}, bf16[1,128,2048]{1,2,0:T(8,128)(2,1)}, u32[]{:S(2)}) copy-start(bf16[1,128,2048]{1,2,0:T(8,128)(2,1)} %copy.114) | copy-start | bytes 1572868 | tf_op jit(solution)/shard_map/while
  225.3 13.5 %copy-start.4 = (bf16[1,128,2048]{1,2,0:T(8,128)(2,1)S(1)}, bf16[1,128,2048]{1,2,0:T(8,128)(2,1)}, u32[]{:S(2)}) copy-start(bf16[1,128,2048]{1,2,0:T(8,128)(2,1)} %copy.113) | copy-start | bytes 1572868 | tf_op jit(solution)/shard_map/while
  238.9 5.0 copy-start.5
  246.4 5.5 copy-start.9
  246.4 5.7 copy-start.8
  253.3 4.8 copy-start.12
  258.2 3.5 copy-start.11
  267.7 2.2 copy-start.3
  268.8 1.1 copy-start.1
  269.9 4.5 copy-start.6
  274.4 7.4 %copy-start.2 = (bf16[1024,512]{0,1:T(8,128)(2,1)S(1)}, bf16[1024,512]{0,1:T(8,128)(2,1)}, u32[]{:S(2)}) copy-start(bf16[1024,512]{0,1:T(8,128)(2,1)} %copy-done.1) | copy-start | bytes 3145732 | tf_op jit(solution)/shard_map/while
  286.8 13.8 %copy-start.7 = (bf16[1,128,2048]{1,2,0:T(8,128)(2,1)S(1)}, bf16[1,128,2048]{1,2,0:T(8,128)(2,1)}, u32[]{:S(2)}) copy-start(bf16[1,128,2048]{1,2,0:T(8,128)(2,1)} %copy.114) | copy-start | bytes 1572868 | tf_op jit(solution)/shard_map/while
  300.5 13.5 %copy-start.4 = (bf16[1,128,2048]{1,2,0:T(8,128)(2,1)S(1)}, bf16[1,128,2048]{1,2,0:T(8,128)(2,1)}, u32[]{:S(2)}) copy-start(bf16[1,128,2048]{1,2,0:T(8,128)(2,1)} %copy.113) | copy-start | bytes 1572868 | tf_op jit(solution)/shard_map/while
  314.1 5.0 copy-start.5
  321.6 5.5 copy-start.9
  321.6 5.7 copy-start.8
  328.5 4.8 copy-start.12
  342.7 172.7 %reduce-scatter.8.cloned.1.call-start = ((), (), s32[]{:S(2)}) async-start(), calls=%async_computation.6 | async-start | bytes 8912896 | tf_op jit(solution)/shard_map/reduce_scatter | solution.py:119
  342.7 7.9 %copy-start.17 = (s32[6]{0:T(128)S(1)}, s32[6]{0:T(128)}, u32[]{:S(2)}) copy-start(s32[6]{0:T(128)} %fusion.40) | copy-start | bytes 76
  368.5 0.7 copy-start.15
  368.5 267.8 %reduce-scatter.10.cloned.1.call-start = ((), (), s32[]{:S(2)}) async-start(), calls=%async_computation.7 | async-start | bytes 13369344
  374.7 6.2 collective-permute-start.2
  377.1 8.6 %collective-permute-start.3 = (bf16[1,128,1024]{2,1,0:T(8,128)(2,1)S(1)}, bf16[1,128,1024]{2,1,0:T(8,128)(2,1)S(1)}, u32[]{:S(2)}, u32[]{:S(2)}) collective-permute-start(bf16[1,128,1024]{2,1,0:T(8,128)(2,1)S(1)} %get-tuple-element.145), channel_id=1, source_target_pairs={{0,8},{8,16},{16,24},{24,32},{32,40},{40,48},{48,56},{56,64},{64,7... | collective-permute-start | bytes 786440 | tf_op jit(solution)/shard_map/ppermute | solution.py:34
  541.5 125.2 %reduce-scatter.12.cloned.1.call-start = ((), (), s32[]{:S(2)}) async-start(), calls=%async_computation.8 | async-start | bytes 884736
Sparse Core Ops, SparseCore 0:
  17.7 73.8 all-gather.1
  94.7 83.3 all-reduce.2
  342.8 84.5 all-reduce.4
  430.7 84.6 reduce-scatter.7
  541.6 94.6 reduce-scatter.9
  638.5 28.0 reduce-scatter.11
where the time goes:
time: 679 us; the launch traced here: 676 us
  waiting for transfers between devices  397 us (58%)
  matrix products  114 us (17%)
  local copies, waits for them, and re-layouts  97 us (14%)
  other arithmetic  44.8 us (7%)
  between operations  14.3 us (2%)
  starting transfers between devices  8.42 us (1%)
    unnamed x8, waiting for transfers between devices  125 us
    reduce_scatter x1, waiting for transfers between devices, body(): lax.psum_scatter(spread.astype(jnp.bfloat16), 'seq', scatter_dimension=1,...  88 us
    psum x1, waiting for transfers between devices, broadcast(): return lax.psum(kept, axis)  76.8 us
    all_gather x1, waiting for transfers between devices, body(): piece = lax.all_gather(kv_local, 'seq', axis=1, tiled=True)  55.9 us
    psum x1, waiting for transfers between devices, body(): lax.psum(jnp.sum(terms[:, :, 3:5], axis=1).astype(jnp.bfloat16), 'seq')  39.7 us
    dot_general x2, matrix products, attend(): jnp.einsum('grqk,kgd->qgrd', dweights, keys, preferred_element_type=jnp.f...  27.5 us
    dot_general x2, matrix products, attend(): jnp.einsum('grqk,qgrd->kgd', dweights, queries, preferred_element_type=jn...  27.1 us
    dynamic_update_slice x10, local copies, waits for them, and re-layouts, body(): lax.map(attend_triple, (query_blocks, picked, grad_blocks))  23.5 us
  transfers between devices with their start and end apart: 10, of which 9 were waited for; matrix products, arithmetic and copies ran while one was open for 8% of the time, Pallas kernels for 0%

commit v1 on v0

v1 whole, which is shorter than its diff:
```python
import functools

import jax
import jax.numpy as jnp
from jax import lax
from jax.experimental import pallas as pl
from jax.experimental.pallas import tpu as pltpu
from jax.sharding import PartitionSpec as P

RING = 4
TOK = 256
BLOCK = 128
D = 2048
HD = 128
GROUP = 4
QW = GROUP * HD
GW = QW + 2 * HD
QBLOCKS = 32
NRAND = 3
SCALE = HD ** -0.5
EXP2_SCALE = SCALE * 1.4426950408889634
BF = jnp.bfloat16
F32 = jnp.float32
MESH = pl.DeviceIdType.MESH
VM = pl.BlockSpec(memory_space=pltpu.VMEM)
HBM = pl.BlockSpec(memory_space=pl.ANY)


def places():
    s, d = lax.axis_index("seq"), lax.axis_index("dp")
    x, y, z, c = s // RING, s % RING, d // 2, d % 2
    return x + c * (y - x), y + c * (x - y), z, c


def shard_of(c, q, r):
    return q * (RING - 3 * c) + r * (1 + 3 * c)


def turn(i, steps):
    return lax.rem(i + steps, RING)


def wait_in(ref, sem):
    pltpu.make_async_copy(ref, ref, sem).wait()


def gather_kernel(x_ref, w_ref, g_ref, xt_out, q_out, g_out, kv_out,
                  xbuf, wbuf, xtbuf, qbuf, kvbuf,
                  local_sem, x_send, x_recv, g_send, g_recv, kv_send, kv_recv, out_sem):
    q, r, z, c = places()

    def peer(q_, r_):
        return (shard_of(c, q_, r_), z * 2 + c)

    rs = [turn(r, k) for k in (1, 3, 2)]
    qs = [turn(q, k) for k in (1, 3, 2)]
    locals_ = [
        pltpu.make_async_copy(x_ref, xbuf.at[r], local_sem.at[0]),
        pltpu.make_async_copy(w_ref.at[:, pl.ds(pl.multiple_of(r * QW, QW), QW)], wbuf.at[:, 0:QW], local_sem.at[1]),
        pltpu.make_async_copy(w_ref.at[:, pl.ds(pl.multiple_of(2048 + r * HD, HD), HD)],
                              wbuf.at[:, QW:QW + HD], local_sem.at[2]),
        pltpu.make_async_copy(w_ref.at[:, pl.ds(pl.multiple_of(2560 + r * HD, HD), HD)],
                              wbuf.at[:, QW + HD:GW], local_sem.at[3]),
        pltpu.make_async_copy(g_ref.at[:, pl.ds(pl.multiple_of(r * QW, QW), QW)], g_out.at[r], local_sem.at[4]),
    ]
    for copy in locals_:
        copy.start()

    barrier = pltpu.get_barrier_semaphore()
    for k in range(3):
        pl.semaphore_signal(barrier, inc=1, device_id=peer(q, rs[k]), device_id_type=MESH)
        pl.semaphore_signal(barrier, inc=1, device_id=peer(qs[k], r), device_id_type=MESH)
    pl.semaphore_wait(barrier, 6)

    def remote(src, dst, send, recv, to):
        copy = pltpu.make_async_remote_copy(src_ref=src, dst_ref=dst, send_sem=send, recv_sem=recv,
                                            device_id=to, device_id_type=MESH)
        copy.start()
        return copy

    up, down, far = rs
    halves = (pl.ds(0, BLOCK), pl.ds(BLOCK, BLOCK))
    sent = []
    for n, (half, to) in enumerate(((0, up), (1, down), (1, up), (0, down))):
        sent.append(remote(x_ref.at[halves[half]], xbuf.at[r, halves[half]], x_send.at[n], x_recv.at[n], peer(q, to)))

    outs = []

    def project(step, j):
        for part in range(3):
            cols = slice(part * 256, (part + 1) * 256)
            got = jnp.dot(xbuf[j], wbuf[:, cols], preferred_element_type=F32).astype(BF)
            if part < 2:
                qbuf[j, :, cols] = got
            else:
                kvbuf[j] = got
        slot = kv_out.at[q * RING + j]
        for k in range(3):
            sent.append(remote(kvbuf.at[j], slot, kv_send.at[step * 3 + k], kv_recv.at[step * 3 + k], peer(qs[k], r)))
        outs.append(pltpu.make_async_copy(kvbuf.at[j], slot, out_sem.at[step * 2]))
        outs[-1].start()
        outs.append(pltpu.make_async_copy(qbuf.at[j], q_out.at[j], out_sem.at[step * 2 + 1]))
        outs[-1].start()

    def transpose(j):
        turned = xbuf[j].T.reshape(RING, RING, RING, 32, TOK)
        xtbuf[:, :, :, :, pl.ds(pl.multiple_of(j * TOK, TOK), TOK)] = turned

    for copy in locals_[:4]:
        copy.wait()
    project(0, r)
    transpose(r)
    wait_in(xbuf.at[down, halves[0]], x_recv.at[0])
    sent.append(remote(xbuf.at[down, halves[0]], xbuf.at[down, halves[0]], x_send.at[4], x_recv.at[4], peer(q, up)))
    wait_in(xbuf.at[up, halves[1]], x_recv.at[1])
    sent.append(remote(xbuf.at[up, halves[1]], xbuf.at[up, halves[1]], x_send.at[5], x_recv.at[5], peer(q, down)))
    wait_in(xbuf.at[down, halves[1]], x_recv.at[2])
    project(1, down)
    wait_in(xbuf.at[up, halves[0]], x_recv.at[3])
    project(2, up)
    for k in range(3):
        sent.append(remote(g_ref.at[:, pl.ds(pl.multiple_of(rs[k] * QW, QW), QW)], g_out.at[r],
                           g_send.at[k], g_recv.at[k], peer(q, rs[k])))
    transpose(down)
    transpose(up)
    wait_in(xbuf.at[far, halves[0]], x_recv.at[4])
    wait_in(xbuf.at[far, halves[1]], x_recv.at[5])
    project(3, far)
    transpose(far)
    outs.append(pltpu.make_async_copy(xtbuf, xt_out, out_sem.at[8]))
    outs[-1].start()

    for step, j in enumerate((r, down, up, far)):
        for k, source in enumerate((qs[1], qs[0], qs[2])):
            wait_in(kv_out.at[source * RING + j], kv_recv.at[step * 3 + k])
    for k, source in enumerate((down, up, far)):
        wait_in(g_out.at[source], g_recv.at[k])
    for copy in sent:
        copy.wait_send()
    for copy in outs + locals_[4:]:
        copy.wait()


def gather(inputs, w_qkv, d_out):
    return pl.pallas_call(
        gather_kernel,
        out_shape=[
            jax.ShapeDtypeStruct((RING, RING, RING, 32, RING * TOK), BF),
            jax.ShapeDtypeStruct((RING, TOK, QW), BF),
            jax.ShapeDtypeStruct((RING, TOK, QW), BF),
            jax.ShapeDtypeStruct((RING * RING, TOK, 2 * HD), BF),
        ],
        in_specs=[HBM] * 3,
        out_specs=[HBM] * 4,
        scratch_shapes=[
            pltpu.VMEM((RING, TOK, D), BF),
            pltpu.VMEM((D, GW), BF),
            pltpu.VMEM((RING, RING, RING, 32, RING * TOK), BF),
            pltpu.VMEM((RING, TOK, QW), BF),
            pltpu.VMEM((RING, TOK, 2 * HD), BF),
            pltpu.SemaphoreType.DMA((5,)),
            pltpu.SemaphoreType.DMA((6,)),
            pltpu.SemaphoreType.DMA((6,)),
            pltpu.SemaphoreType.DMA((3,)),
            pltpu.SemaphoreType.DMA((3,)),
            pltpu.SemaphoreType.DMA((12,)),
            pltpu.SemaphoreType.DMA((12,)),
            pltpu.SemaphoreType.DMA((9,)),
        ],
        compiler_params=pltpu.CompilerParams(collective_id=1, has_side_effects=True, vmem_limit_bytes=40 * 2**20),
        cost_estimate=pl.CostEstimate(flops=2 * 1024 * D * GW, bytes_accessed=20 * 2**20, transcendentals=0),
        name="gather_project",
    )(inputs, w_qkv, d_out)


def attend_kernel(rb, q_ref, g_ref, kv_ref, att_ref, dq_ref, dkv_ref, kcat, acc):
    q, r, z, c = places()
    i = pl.program_id(0)
    b = shard_of(c, q, i // 2) * 2 + i % 2

    @pl.when(i == 0)
    def _():
        acc[...] = jnp.zeros_like(acc)

    listed = [lax.rem(b + QBLOCKS - 1, QBLOCKS), b, lax.rem(b + 1, QBLOCKS), jnp.int32(0), jnp.int32(1)]
    listed += [rb[b, n] for n in range(NRAND)]

    def slot(n):
        s = n // 2
        return (s + c * ((s % RING) * RING + s // RING - s)) * 2 + n % 2

    ids = [slot(n) for n in listed]
    for l, n in enumerate(ids):
        kcat[pl.ds(l * BLOCK, BLOCK), :] = kv_ref[n]
    keys, values = kcat[:, :HD], kcat[:, HD:]
    heads = [slice(h * HD, (h + 1) * HD) for h in range(GROUP)]
    queries = jnp.concatenate([q_ref[0, :, h] for h in heads], axis=0)
    grads = jnp.concatenate([g_ref[0, :, h] for h in heads], axis=0)
    nt = (((1,), (1,)), ((), ()))
    scores = lax.dot_general(keys, queries, nt, preferred_element_type=F32)
    peak = jnp.max(scores, axis=0, keepdims=True)
    expos = jnp.exp2((scores - peak) * EXP2_SCALE)
    probs = expos * (1.0 / jnp.sum(expos, axis=0, keepdims=True))
    weights = probs.astype(BF)
    dprob = lax.dot_general(values, grads, nt, preferred_element_type=F32)
    attended = jnp.dot(values.T, weights, preferred_element_type=F32)
    mean = jnp.sum(probs * dprob, axis=0, keepdims=True)
    dweights = (probs * (dprob - mean) * SCALE).astype(BF)
    d_query = jnp.dot(keys.T, dweights, preferred_element_type=F32)
    for h in heads:
        att_ref[0, :, h] = attended[:, h].T.astype(BF)
        dq_ref[0, :, h] = d_query[:, h].T.astype(BF)
    d_key = jnp.dot(dweights, queries, preferred_element_type=F32)
    d_value = jnp.dot(weights, grads, preferred_element_type=F32)
    for l, n in enumerate(ids):
        rows = slice(l * BLOCK, (l + 1) * BLOCK)
        acc[n, :, 0:HD] += d_key[rows]
        acc[n, :, HD:] += d_value[rows]

    @pl.when(i == 7)
    def _():
        dkv_ref[...] = acc[...].astype(BF)


def attend(random_blocks, queries, grads, kv):
    whole = lambda i, *_: (0, 0, 0)
    block = pl.BlockSpec((1, BLOCK, QW), lambda i, *_: (i, 0, 0))
    return pl.pallas_call(
        attend_kernel,
        grid_spec=pltpu.PrefetchScalarGridSpec(
            num_scalar_prefetch=1,
            grid=(2 * RING,),
            in_specs=[block, block, pl.BlockSpec((QBLOCKS, BLOCK, 2 * HD), whole)],
            out_specs=[block, block, pl.BlockSpec((QBLOCKS, BLOCK, 2 * HD), whole)],
            scratch_shapes=[pltpu.VMEM((8 * BLOCK, 2 * HD), BF), pltpu.VMEM((QBLOCKS, BLOCK, 2 * HD), F32)],
        ),
        out_shape=[
            jax.ShapeDtypeStruct((2 * RING, BLOCK, QW), BF),
            jax.ShapeDtypeStruct((2 * RING, BLOCK, QW), BF),
            jax.ShapeDtypeStruct((QBLOCKS, BLOCK, 2 * HD), BF),
        ],
        compiler_params=pltpu.CompilerParams(vmem_limit_bytes=48 * 2**20),
        cost_estimate=pl.CostEstimate(flops=12 * 2**29, bytes_accessed=8 * 2**20, transcendentals=2**22),
        name="attend",
    )(random_blocks, queries.reshape(2 * RING, BLOCK, QW), grads.reshape(2 * RING, BLOCK, QW),
      kv.reshape(QBLOCKS, BLOCK, 2 * HD))


def reduce_kernel(xt_ref, dq_ref, dkv_ref, att_ref, att_out, dw_out,
                  xt, dq, dkv_own, dkv_in, dkv, zs, zin, qs_, qin, ks, kin, kzs, kzin, fs, fin,
                  local_sem, dkv_send, dkv_recv, att_send, att_recv, z_send, z_recv, q_send, q_recv,
                  k_send, k_recv, kz_send, kz_recv, f_send, f_recv):
    q, r, z, c = places()
    order = (1, 3, 2)
    rs = [turn(r, k) for k in order]
    qs = [turn(q, k) for k in order]
    zz = [turn(z, k) for k in order]
    back = (1, 0, 2)

    def peer(q_, r_, z_):
        return (shard_of(c, q_, r_), z_ * 2 + c)

    @pl.when(c == 0)
    def _():
        for i in range(RING):
            pltpu.make_async_copy(xt_ref.at[i, :, :], xt.at[i], local_sem.at[0]).start()

    @pl.when(c == 1)
    def _():
        for i in range(RING):
            pltpu.make_async_copy(xt_ref.at[:, i, :], xt.at[i], local_sem.at[0]).start()

    load_dq = pltpu.make_async_copy(dq_ref, dq, local_sem.at[1])
    load_dq.start()
    load_dkv = pltpu.make_async_copy(dkv_ref.at[pl.ds(q * RING, RING)], dkv_own, local_sem.at[2])
    load_dkv.start()
    own_att = pltpu.make_async_copy(att_ref.at[r], att_out.at[:, pl.ds(pl.multiple_of(r * QW, QW), QW)], local_sem.at[3])
    own_att.start()

    barrier = pltpu.get_barrier_semaphore()
    met = [peer(q, rs[k], z) for k in range(3)] + [peer(qs[k], r, z) for k in range(3)]
    met += [peer(q, r, zz[k]) for k in range(3)]
    met += [(shard_of(c, q, turn(r, k)), z * 2 + 1 - c) for k in range(RING)]
    met += [(shard_of(c, turn(q, k), r), z * 2 + 1 - c) for k in range(RING)]
    for device in met:
        pl.semaphore_signal(barrier, inc=1, device_id=device, device_id_type=MESH)
    pl.semaphore_wait(barrier, len(met))

    sent = []

    def remote(src, dst, send, recv, to):
        copy = pltpu.make_async_remote_copy(src_ref=src, dst_ref=dst, send_sem=send, recv_sem=recv,
                                            device_id=to, device_id_type=MESH)
        copy.start()
        sent.append(copy)

    for k in range(3):
        remote(dkv_ref.at[pl.ds(qs[k] * RING, RING)], dkv_in.at[k], dkv_send.at[k], dkv_recv.at[k], peer(qs[k], r, z))
    for k in range(3):
        remote(att_ref.at[rs[k]], att_out.at[:, pl.ds(pl.multiple_of(r * QW, QW), QW)],
               att_send.at[k], att_recv.at[k], peer(q, rs[k], z))

    load_dq.wait()
    wait_in(xt, local_sem.at[0])
    dq_all = dq[...].reshape(RING * TOK, QW)

    def rows_of(z_, q_):
        return xt[q_, :, z_].reshape(RING * 32, RING * TOK)

    for k in (2, 0, 1):
        for q_ in range(RING):
            zs[k, q_] = jnp.dot(rows_of(zz[k], q_), dq_all, preferred_element_type=F32).astype(BF)
        remote(zs.at[k], zin.at[k], z_send.at[k], z_recv.at[k], peer(q, r, zz[k]))
    own_z = [jnp.dot(rows_of(z, q_), dq_all, preferred_element_type=F32) for q_ in range(RING)]
    for q_ in range(RING):
        zs[3, q_] = own_z[q_].astype(BF)

    load_dkv.wait()
    for k in range(3):
        wait_in(dkv_in.at[k], dkv_recv.at[k])
    total = dkv_own[...].astype(F32)
    for k in range(3):
        total += dkv_in[k].astype(F32)
    dkv[...] = total.astype(BF)
    dkv_all = dkv[...].reshape(RING * TOK, 2 * HD)
    for k in (2, 0, 1):
        for z_ in range(RING):
            ks[k, z_] = jnp.dot(rows_of(z_, qs[k]), dkv_all, preferred_element_type=F32).astype(BF)
        remote(ks.at[k], kin.at[k], k_send.at[k], k_recv.at[k], peer(qs[k], r, z))
    for z_ in range(RING):
        ks[3, z_] = jnp.dot(rows_of(z_, q), dkv_all, preferred_element_type=F32).astype(BF)
    for k in range(3):
        wait_in(kin.at[k], k_recv.at[k])
    for k in range(3):
        got = ks[3, zz[k]].astype(F32)
        for n in range(3):
            got += kin[n, zz[k]].astype(F32)
        kzs[k] = got.astype(BF)
        remote(kzs.at[k], kzin.at[k], kz_send.at[k], kz_recv.at[k], peer(q, r, zz[k]))

    for k in range(3):
        wait_in(zin.at[k], z_recv.at[k])
    for k in range(3):
        got = zs[3, qs[k]].astype(F32)
        for n in range(3):
            got += zin[n, qs[k]].astype(F32)
        qs_[k] = got.astype(BF)
        remote(qs_.at[k], qin.at[k], q_send.at[k], q_recv.at[k], peer(qs[k], r, z))
    own_q = zs[3, q].astype(F32)
    own_k = ks[3, z].astype(F32)
    for n in range(3):
        own_q += zin[n, q].astype(F32)
        own_k += kin[n, z].astype(F32)
    for k in range(3):
        wait_in(qin.at[k], q_recv.at[k])
        wait_in(kzin.at[k], kz_recv.at[k])
    for k in range(3):
        own_q += qin[k].astype(F32)
        own_k += kzin[k].astype(F32)
    fs[:, :, :, 0:QW] = own_q.astype(BF).reshape(RING, 2, 16, QW)
    fs[:, :, :, QW:GW] = own_k.astype(BF).reshape(RING, 2, 16, 2 * HD)

    for k in range(RING):
        to = turn(r, k)
        if k:
            remote(fs.at[to, c], fin.at[0, k], f_send.at[k], f_recv.at[k], (shard_of(c, q, to), z * 2 + c))
        remote(fs.at[to, 1 - c], fin.at[1, k], f_send.at[RING + k], f_recv.at[RING + k],
               (shard_of(c, q, to), z * 2 + 1 - c))
    fin[0, 0] = fs[r, c]
    for k in range(RING):
        if k:
            wait_in(fin.at[0, k], f_recv.at[k])
        wait_in(fin.at[1, k], f_recv.at[RING + k])
    for g in range(RING):
        mine = fin[0, lax.rem(r + RING - g, RING)].astype(F32)
        other = fin[1, lax.rem(q + RING - g, RING)].astype(F32)
        got = mine + other
        dw_out[:, g * QW:(g + 1) * QW] = got[:, 0:QW]
        dw_out[:, 2048 + g * HD:2048 + (g + 1) * HD] = got[:, QW:QW + HD]
        dw_out[:, 2560 + g * HD:2560 + (g + 1) * HD] = got[:, QW + HD:GW]

    for k in range(3):
        wait_in(att_out.at[:, pl.ds(pl.multiple_of(rs[back[k]] * QW, QW), QW)], att_recv.at[k])
    for copy in sent:
        copy.wait_send()
    own_att.wait()


def reduce(xt, d_query, d_kv, attended):
    dma = pltpu.SemaphoreType.DMA
    return pl.pallas_call(
        reduce_kernel,
        out_shape=[jax.ShapeDtypeStruct((TOK, D), BF), jax.ShapeDtypeStruct((16, RING * GW), F32)],
        in_specs=[HBM] * 4,
        out_specs=[HBM, VM],
        scratch_shapes=[
            pltpu.VMEM((RING, RING, RING, 32, RING * TOK), BF),
            pltpu.VMEM((RING, TOK, QW), BF),
            pltpu.VMEM((RING, TOK, 2 * HD), BF),
            pltpu.VMEM((3, RING, TOK, 2 * HD), BF),
            pltpu.VMEM((RING, TOK, 2 * HD), BF),
            pltpu.VMEM((4, RING, 128, QW), BF),
            pltpu.VMEM((3, RING, 128, QW), BF),
            pltpu.VMEM((3, 128, QW), BF),
            pltpu.VMEM((3, 128, QW), BF),
            pltpu.VMEM((4, RING, 128, 2 * HD), BF),
            pltpu.VMEM((3, RING, 128, 2 * HD), BF),
            pltpu.VMEM((3, 128, 2 * HD), BF),
            pltpu.VMEM((3, 128, 2 * HD), BF),
            pltpu.VMEM((RING, 2, 16, GW), BF),
            pltpu.VMEM((2, RING, 16, GW), BF),
            dma((4,)), dma((3,)), dma((3,)), dma((3,)), dma((3,)), dma((3,)), dma((3,)), dma((3,)), dma((3,)),
            dma((3,)), dma((3,)), dma((3,)), dma((3,)), dma((8,)), dma((8,)),
        ],
        compiler_params=pltpu.CompilerParams(collective_id=2, has_side_effects=True, vmem_limit_bytes=40 * 2**20),
        cost_estimate=pl.CostEstimate(flops=2 * 1024 * D * GW, bytes_accessed=12 * 2**20, transcendentals=0),
        name="weight_gradient",
    )(xt, d_query.reshape(RING, TOK, QW), d_kv.reshape(RING * RING, TOK, 2 * HD), attended.reshape(RING, TOK, QW))


def body(inputs, w_qkv, random_blocks, d_out):
    xt, queries, grads, kv = gather(inputs[0], w_qkv, d_out[0])
    attended, d_query, d_kv = attend(random_blocks, queries, grads, kv)
    attended, d_wqkv = reduce(xt, d_query, d_kv, attended)
    return attended[None], d_wqkv


def solution(mesh):
    return jax.shard_map(
        body,
        mesh=mesh,
        in_specs=(P("dp", "seq", None), P(), P(), P("dp", "seq", None)),
        out_specs=(P("dp", "seq", None), P(("seq", "dp"), None)),
        check_vma=False,
    )
```

time: 679 us -> 119 us (0.18)
  waiting for transfers between devices: 397 us -> 0 us
  matrix products: 114 us -> 0 us
  Pallas kernels: 0 us -> 110 us
  local copies, waits for them, and re-layouts: 97 us -> 7.8 us
  other arithmetic: 44.8 us -> 0 us
  between operations: 14.3 us -> 0.66 us
  starting transfers between devices: 8.42 us -> 0 us
    unnamed x8 -> x0, waiting for transfers between devices: 125 us -> none
    psum x2 -> x0, waiting for transfers between devices: 117 us -> none  [the longest x1 76.8 us: broadcast(): return lax.psum(kept, axis)]
    pallas_call x0 -> x3, Pallas kernels: none -> 110 us  [the longest x1 44.3 us: reduce(): pl.pallas_call(reduce_kernel, out_shape=[jax.ShapeDtypeStruct((TOK, D), B...]
    dot_general x12 -> x0, matrix products: 99.2 us -> none  [the longest x2 27.5 us: attend(): jnp.einsum('grqk,kgd->qgrd', dweights, keys, preferred_element_type=jnp.f...]
    reduce_scatter x1 -> x0, waiting for transfers between devices: 88 us -> none  [body(): lax.psum_scatter(spread.astype(jnp.bfloat16), 'seq', scatter_dimension=1,...]
    all_gather x1 -> x0, waiting for transfers between devices: 55.9 us -> none  [body(): piece = lax.all_gather(kv_local, 'seq', axis=1, tiled=True)]
    dynamic_update_slice x10 -> x0, local copies, waits for them, and re-layouts: 23.5 us -> none  [body(): lax.map(attend_triple, (query_blocks, picked, grad_blocks))]
    dynamic_slice x13 -> x0, local copies, waits for them, and re-layouts: 19.1 us -> none  [the longest x12 19 us: body(): lax.map(attend_triple, (query_blocks, picked, grad_blocks))]
  transfers between devices with their start and end apart: 10 -> 0, of which waited for: 9 -> 0; matrix products, arithmetic and copies ran while one was open for 8% -> 0% of each run, Pallas kernels for 0% -> 0%
where the time goes in v1:
time: 119 us; the launch traced here: 118 us
  Pallas kernels  110 us (92%)
  local copies, waits for them, and re-layouts  7.8 us (7%)
    pallas_call x1, Pallas kernels, reduce(): pl.pallas_call(reduce_kernel, out_shape=[jax.ShapeDtypeStruct((TOK, D), B...  44.3 us
    pallas_call x1, Pallas kernels, gather(): pl.pallas_call(gather_kernel, out_shape=[jax.ShapeDtypeStruct((RING, RING...  42.4 us
    pallas_call x1, Pallas kernels, attend(): pl.pallas_call(attend_kernel, grid_spec=pltpu.PrefetchScalarGridSpec(num_...  23.3 us
    unnamed x11, local copies, waits for them, and re-layouts  7.8 us

profile of v1, /device:TPU:1, one launch (start us, length us, event | category | flops | bytes accessed | tf_op | source)
XLA Modules:
  0.0 118.5 jit_solution(10314388350802736429)
XLA Ops:
  0.6 0.8 copy.6.rb
  1.4 0.0 copy-start
  1.4 1.2 %copy-done = bf16[1,256,2048]{2,1,0:T(8,128)(2,1)S(1)} copy-done((bf16[1,256,2048]{2,1,0:T(8,128)(2,1)S(1)}, bf16[1,256,2048]{2,1,0:T(8,128)(2,1)}, u32[]{:S(2)}) %copy-start) | copy-done | bytes 1048600
  2.6 0.0 copy-start.1
  2.6 1.2 %copy-done.1 = bf16[1,256,2048]{2,1,0:T(8,128)(2,1)S(1)} copy-done((bf16[1,256,2048]{2,1,0:T(8,128)(2,1)S(1)}, bf16[1,256,2048]{2,1,0:T(8,128)(2,1)}, u32[]{:S(2)}) %copy-start.1) | copy-done | bytes 1048600
  3.8 42.4 %gather_project.1 = (bf16[4,4,4,32,1024]{4,3,2,1,0:T(8,128)(2,1)S(1)}, bf16[4,256,512]{2,1,0:T(8,128)(2,1)S(1)}, bf16[4,256,512]{2,1,0:T(8,128)(2,1)S(1)}, bf16[16,256,256]{2,1,0:T(8,128)(2,1)S(1)}) custom-call(bf16[256,2048]{1,0:T(8,128)(2,1)S(1)} %bitcast.9, bf16[2048,3072]{1,0:T(8,128)(2,1)} %w_ref.1, bf16[256,2048]{1,0:T(8,128)(2,1)S(1)} %bitcast.10), custom_call_target="tpu_custom_call" | custom-call | flops 3221225472 | bytes 20971520 | tf_op jit(solution)/shard_map/gather_project/pallas_call | solution.py:145
  46.3 0.0 copy-start.2
  46.3 1.3 %copy-done.2 = bf16[16,256,256]{2,1,0:T(8,128)(2,1)} copy-done((bf16[16,256,256]{2,1,0:T(8,128)(2,1)}, bf16[16,256,256]{2,1,0:T(8,128)(2,1)S(1)}, u32[]{:S(2)}) %copy-start.2) | copy-done | bytes 2097176
  47.7 23.3 %attend.1 = (bf16[8,128,512]{2,1,0:T(8,128)(2,1)S(1)}, bf16[8,128,512]{2,1,0:T(8,128)(2,1)S(1)}, bf16[32,128,256]{2,1,0:T(8,128)(2,1)}) custom-call(s32[32,3]{1,0:T(8,128)S(1)} %copy.6.rb, bf16[8,128,512]{2,1,0:T(8,128)(2,1)S(1)} %bitcast.13, bf16[8,128,512]{2,1,0:T(8,128)(2,1)S(1)} %bitcast.14, bf16[32,128,256]{2,1,0:T(8,128)(2,1)} %bitcast.12), custom_call_target="tpu_custom_call" | custom-call | flops 6442450944 | bytes 8388608 | tf_op jit(solution)/shard_map/attend/pallas_call | solution.py:228
  70.9 0.0 copy-start.3
  70.9 1.6 %copy-done.3 = bf16[32,128,256]{2,1,0:T(8,128)(2,1)S(1)} copy-done((bf16[32,128,256]{2,1,0:T(8,128)(2,1)S(1)}, bf16[32,128,256]{2,1,0:T(8,128)(2,1)}, u32[]{:S(2)}) %copy-start.3) | copy-done | bytes 2097176
  72.5 44.3 %weight_gradient.1 = (bf16[256,2048]{1,0:T(8,128)(2,1)S(1)}, f32[16,3072]{1,0:T(8,128)S(1)}) custom-call(bf16[4,4,4,32,1024]{4,3,2,1,0:T(8,128)(2,1)S(1)} %get-tuple-element.11.xt_ref, bf16[4,256,512]{2,1,0:T(8,128)(2,1)S(1)} %bitcast.17, bf16[16,256,256]{2,1,0:T(8,128)(2,1)S(1)} %bitcast.15, bf16[4,256,512]{2,1,0:T(8,128)(2,1)S(1)} %bitcast.16), custom_call_target="tpu_custom_call" | custom-call | flops 3221225472 | bytes 12582912 | tf_op jit(solution)/shard_map/weight_gradient/pallas_call | solution.py:391
  116.8 1.0 copy.9
  117.8 0.7 copy.10
Async XLA Ops:
  1.4 1.2 %copy-start = (bf16[1,256,2048]{2,1,0:T(8,128)(2,1)S(1)}, bf16[1,256,2048]{2,1,0:T(8,128)(2,1)}, u32[]{:S(2)}) copy-start(bf16[1,256,2048]{2,1,0:T(8,128)(2,1)} %param.4) | copy-start | bytes 3145732
  2.6 1.2 %copy-start.1 = (bf16[1,256,2048]{2,1,0:T(8,128)(2,1)S(1)}, bf16[1,256,2048]{2,1,0:T(8,128)(2,1)}, u32[]{:S(2)}) copy-start(bf16[1,256,2048]{2,1,0:T(8,128)(2,1)} %param.7) | copy-start | bytes 3145732
  46.3 1.4 %copy-start.2 = (bf16[16,256,256]{2,1,0:T(8,128)(2,1)}, bf16[16,256,256]{2,1,0:T(8,128)(2,1)S(1)}, u32[]{:S(2)}) copy-start(bf16[16,256,256]{2,1,0:T(8,128)(2,1)S(1)} %get-tuple-element.14) | copy-start | bytes 6291460
  70.9 1.6 %copy-start.3 = (bf16[32,128,256]{2,1,0:T(8,128)(2,1)S(1)}, bf16[32,128,256]{2,1,0:T(8,128)(2,1)}, u32[]{:S(2)}) copy-start(bf16[32,128,256]{2,1,0:T(8,128)(2,1)} %get-tuple-element.16) | copy-start | bytes 6291460

commit v2 on v0

v2 whole, which is shorter than its diff:
```python
import jax
import jax.numpy as jnp
from jax import lax
from jax.experimental import pallas as pl
from jax.experimental.pallas import tpu as pltpu
from jax.sharding import PartitionSpec as P

RING = 4
TOK = 256
BLOCK = 128
D = 2048
HD = 128
GROUP = 4
QW = GROUP * HD
KV = 2 * HD
GW = QW + KV
QBLOCKS = 32
NRAND = 3
LOCAL = 2 * RING
PICKS = LOCAL * NRAND
SCALE = HD ** -0.5
EXP2_SCALE = SCALE * 1.4426950408889634
BF = jnp.bfloat16
F32 = jnp.float32
MESH = pl.DeviceIdType.MESH


def places():
    s, d = lax.axis_index("seq"), lax.axis_index("dp")
    x, y, z, c = s // RING, s % RING, d // 2, d % 2
    return x + c * (y - x), y + c * (x - y), z, c


def shard_of(c, q, r):
    return q * (RING - 3 * c) + r * (1 + 3 * c)


def turn(i, steps):
    return lax.rem(i + steps, RING)


def wait_in(ref, sem):
    pltpu.make_async_copy(ref, ref, sem).wait()


def dot(a, b):
    return jnp.dot(a, b, preferred_element_type=F32)


def kernel(rb, x_ref, w_ref, g_ref, att_out, dw_out,
           xall, wkv, wq, kvown, qown, kvall, qall, gall, attb, dqb, near, terms, kcat, ids, prev, last,
           xt, dkvs, dkv_in, dkv, zs, zin, qs_, qin, ks, kin, kzs, kzin, fs, fin,
           local_sem, wq_sem, a_send, a_recv, kv_send, kv_recv, q_send, q_recv, g_send, g_recv, x_send, x_recv,
           dkv_send, dkv_recv, att_send, att_recv, z_send, z_recv, dq_send, dq_recv, k_send, k_recv, kz_send, kz_recv,
           f_send, f_recv):
    q, r, z, c = places()
    rs = [turn(r, k) for k in (1, 3, 2)]
    qs = [turn(q, k) for k in (1, 3, 2)]
    zz = [turn(z, k) for k in (1, 3, 2)]
    up, down, far = rs
    r_from = (down, up, far)
    q_from = (qs[1], qs[0], qs[2])

    def peer(q_, r_, z_):
        return (shard_of(c, q_, r_), z_ * 2 + c)

    load_x = pltpu.make_async_copy(x_ref, xall.at[r], local_sem.at[0])
    load_x.start()
    load_wkv = pltpu.make_async_copy(w_ref.at[:, pl.ds(RING * QW, RING * KV)], wkv, local_sem.at[1])
    load_wkv.start()
    load_g = pltpu.make_async_copy(g_ref.at[:, pl.ds(pl.multiple_of(r * QW, QW), QW)], gall.at[r], local_sem.at[2])
    load_wq = [pltpu.make_async_copy(w_ref.at[:, pl.ds(pl.multiple_of(to * QW, QW), QW)], wq.at[k], wq_sem.at[k])
               for k, to in enumerate((up, down, far, r))]

    barrier = pltpu.get_barrier_semaphore()
    met = [peer(q, rs[k], z) for k in range(3)] + [peer(qs[k], r, z) for k in range(3)]
    met += [peer(q, r, zz[k]) for k in range(3)]
    met += [(shard_of(c, q, turn(r, k)), z * 2 + 1 - c) for k in range(RING)]
    met += [(shard_of(c, turn(q, k), r), z * 2 + 1 - c) for k in range(RING)]
    for device in met:
        pl.semaphore_signal(barrier, inc=1, device_id=device, device_id_type=MESH)

    sent = []

    def remote(src, dst, send, recv, to):
        copy = pltpu.make_async_remote_copy(src_ref=src, dst_ref=dst, send_sem=send, recv_sem=recv,
                                            device_id=to, device_id_type=MESH)
        sent.append(copy)
        return copy

    load_x.wait()
    load_wkv.wait()
    for copy in load_wq:
        copy.start()
    load_g.start()
    x_own = xall[r]
    for part in range(4):
        got = dot(x_own, wkv[:, part * 256:(part + 1) * 256]).astype(BF)
        cols = slice(0, HD) if part < 2 else slice(HD, KV)
        for n in range(2):
            kvown[part % 2 * 2 + n, :, :, cols] = got[:, n * HD:(n + 1) * HD].reshape(2, BLOCK, HD)
    pl.semaphore_wait(barrier, len(met))

    def slot(j):
        return kvall.at[pl.ds((q * RING + j) * 2, 2)]

    for k in range(3):
        remote(kvown.at[rs[k]], slot(r), a_send.at[k], a_recv.at[k], peer(q, rs[k], z)).start()

    def pass_on(step, src, j):
        for k in range(3):
            remote(src, slot(j), kv_send.at[step * 3 + k], kv_recv.at[step * 3 + k], peer(qs[k], r, z)).start()

    pass_on(0, kvown.at[r], r)
    kvall[pl.ds((q * RING + r) * 2, 2)] = kvown[r]

    for k in range(4):
        load_wq[k].wait()
        for part in range(2):
            cols = slice(part * 256, (part + 1) * 256)
            got = dot(x_own, wq[k, :, cols]).astype(BF)
            if k < 3:
                qown[k, :, cols] = got
            else:
                qall[r, :, cols] = got

    for k, j in enumerate(r_from):
        wait_in(slot(j), a_recv.at[k])
        pass_on(k + 1, slot(j), j)

    def step_j(step):
        return turn(r, jnp.where(step == 0, 0, jnp.where(step == 1, 3, step - 1)))

    def place_of(n):
        s = n // 2
        return (s + c * ((s % RING) * RING + s // RING - s)) * 2 + n % 2

    def fill_ids(i, _):
        b = shard_of(c, q, step_j(i // 2)) * 2 + i % 2
        for n in range(NRAND):
            ids[i * NRAND + n] = place_of(rb[b, n])
        return 0

    lax.fori_loop(0, LOCAL, fill_ids, 0)

    def fill_prev(k, _):
        mine = ids[k]
        got = jnp.int32(PICKS)
        for n in range(PICKS):
            got = jnp.where((ids[n] == mine) & (n < k), n, got)
        prev[k] = got
        return 0

    lax.fori_loop(0, PICKS, fill_prev, 0)

    def fill_last(n, _):
        got = jnp.int32(PICKS)
        for k in range(PICKS):
            got = jnp.where(ids[k] == n, k, got)
        last[n] = got
        return 0

    lax.fori_loop(0, QBLOCKS, fill_last, 0)
    near[...] = jnp.zeros_like(near)
    terms[PICKS] = jnp.zeros((BLOCK, KV), F32)

    def transpose(j):
        turned = xall[j].T.reshape(RING * RING, RING, 32, TOK)
        xt[:, :, :, pl.ds(pl.multiple_of(j * TOK, TOK), TOK)] = turned

    transpose(r)

    q_copies, g_copies = [], []
    for k in range(3):
        q_copies.append(remote(qown.at[k], qall.at[r], q_send.at[k], q_recv.at[k], peer(q, rs[k], z)))
        g_copies.append(remote(g_ref.at[:, pl.ds(pl.multiple_of(rs[k] * QW, QW), QW)], gall.at[r],
                               g_send.at[k], g_recv.at[k], peer(q, rs[k], z)))
    halves = (pl.ds(0, BLOCK), pl.ds(BLOCK, BLOCK))
    x_copies = [remote(xall.at[r, halves[half]], xall.at[r, halves[half]], x_send.at[n], x_recv.at[n], peer(q, to, z))
                for n, (half, to) in enumerate(((0, up), (1, down), (1, up), (0, down)))]
    x_on = [remote(xall.at[down, halves[0]], xall.at[down, halves[0]], x_send.at[4], x_recv.at[4], peer(q, up, z)),
            remote(xall.at[up, halves[1]], xall.at[up, halves[1]], x_send.at[5], x_recv.at[5], peer(q, down, z))]

    for step, j in enumerate((r, down, up, far)):
        for k in range(3):
            wait_in(kvall.at[pl.ds((q_from[k] * RING + j) * 2, 2)], kv_recv.at[step * 3 + k])
    load_g.wait()
    for k in range(3):
        q_copies[k].start()
        g_copies[k].start()

    def attend(i, _):
        @pl.when(i == 1)
        def _():
            for copy in x_copies:
                copy.start()

        for k in range(3):
            @pl.when(i == 2 * k + 2)
            def _():
                wait_in(qall.at[r_from[k]], q_recv.at[k])
                wait_in(gall.at[r_from[k]], g_recv.at[k])

        @pl.when(i == 7)
        def _():
            wait_in(xall.at[down, halves[0]], x_recv.at[0])
            x_on[0].start()
            wait_in(xall.at[up, halves[1]], x_recv.at[1])
            x_on[1].start()

        j = step_j(i // 2)
        b = shard_of(c, q, j) * 2 + i % 2
        rows = pl.ds(pl.multiple_of((i % 2) * BLOCK, BLOCK), BLOCK)
        near_ids = [place_of(n) for n in (lax.rem(b + QBLOCKS - 1, QBLOCKS), b, lax.rem(b + 1, QBLOCKS),
                                          jnp.int32(0), jnp.int32(1))]
        listed = near_ids + [ids[i * NRAND + n] for n in range(NRAND)]
        for l, n in enumerate(listed):
            kcat[pl.ds(l * BLOCK, BLOCK), :] = kvall[n]
        keys, values = kcat[:, :HD], kcat[:, HD:]
        heads = [slice(h * HD, (h + 1) * HD) for h in range(GROUP)]
        queries = jnp.concatenate([qall[j, rows, h] for h in heads], axis=0)
        grads = jnp.concatenate([gall[j, rows, h] for h in heads], axis=0)
        nt = (((1,), (1,)), ((), ()))
        scores = lax.dot_general(keys, queries, nt, preferred_element_type=F32)
        peak = jnp.max(scores, axis=0, keepdims=True)
        expos = jnp.exp2((scores - peak) * EXP2_SCALE)
        probs = expos * (1.0 / jnp.sum(expos, axis=0, keepdims=True))
        weights = probs.astype(BF)
        dprob = lax.dot_general(values, grads, nt, preferred_element_type=F32)
        attended = dot(values.T, weights)
        mean = jnp.sum(probs * dprob, axis=0, keepdims=True)
        dweights = (probs * (dprob - mean) * SCALE).astype(BF)
        d_query = dot(keys.T, dweights)
        for h in heads:
            attb[j, rows, h] = attended[:, h].T.astype(BF)
            dqb[j, rows, h] = d_query[:, h].T.astype(BF)
        d_key = dot(dweights, queries)
        d_value = dot(weights, grads)
        for l, n in enumerate(near_ids):
            at = slice(l * BLOCK, (l + 1) * BLOCK)
            near[n, :, 0:HD] += d_key[at]
            near[n, :, HD:] += d_value[at]
        for l in range(NRAND):
            at = slice((5 + l) * BLOCK, (6 + l) * BLOCK)
            k = i * NRAND + l
            before = terms[prev[k]]
            terms[k, :, 0:HD] = before[:, 0:HD] + d_key[at]
            terms[k, :, HD:] = before[:, HD:] + d_value[at]
        return 0

    lax.fori_loop(0, LOCAL, attend, 0)

    for k in range(3):
        def gather_terms(n, _):
            at = qs[k] * LOCAL + n
            dkvs[at] = (near[at] + terms[last[at]]).astype(BF)
            return 0

        lax.fori_loop(0, LOCAL, gather_terms, 0)
        remote(dkvs.at[pl.ds(qs[k] * LOCAL, LOCAL)], dkv_in.at[k], dkv_send.at[k], dkv_recv.at[k],
               peer(qs[k], r, z)).start()

    wait_in(xall.at[down, halves[1]], x_recv.at[2])
    transpose(down)
    wait_in(xall.at[up, halves[0]], x_recv.at[3])
    transpose(up)
    wait_in(xall.at[far, halves[0]], x_recv.at[4])
    wait_in(xall.at[far, halves[1]], x_recv.at[5])
    transpose(far)
    dq_all = dqb[...].reshape(RING * TOK, QW)

    def rows_of(z_, q_):
        return jnp.concatenate([xt[shard_of(c, q_, n), z_] for n in range(RING)], axis=0)

    for k in (2, 0, 1):
        for q_ in range(RING):
            zs[k, q_] = dot(rows_of(zz[k], q_), dq_all).astype(BF)
        remote(zs.at[k], zin.at[k], z_send.at[k], z_recv.at[k], peer(q, r, zz[k])).start()
    for q_ in range(RING):
        zs[3, q_] = dot(rows_of(z, q_), dq_all).astype(BF)

    for k in range(3):
        wait_in(dkv_in.at[k], dkv_recv.at[k])

    def add_terms(n, _):
        at = q * LOCAL + n
        got = near[at] + terms[last[at]]
        for k in range(3):
            got += dkv_in[k, n].astype(F32)
        dkv[n] = got.astype(BF)
        return 0

    lax.fori_loop(0, LOCAL, add_terms, 0)
    dkv_all = dkv[...].reshape(RING * TOK, KV)
    for k in (2, 0, 1):
        for z_ in range(RING):
            ks[k, z_] = dot(rows_of(z_, qs[k]), dkv_all).astype(BF)
        remote(ks.at[k], kin.at[k], k_send.at[k], k_recv.at[k], peer(qs[k], r, z)).start()
    for k in range(3):
        remote(attb.at[rs[k]], att_out.at[:, pl.ds(pl.multiple_of(r * QW, QW), QW)],
               att_send.at[k], att_recv.at[k], peer(q, rs[k], z)).start()
    own_att = pltpu.make_async_copy(attb.at[r], att_out.at[:, pl.ds(pl.multiple_of(r * QW, QW), QW)], local_sem.at[3])
    own_att.start()
    for z_ in range(RING):
        ks[3, z_] = dot(rows_of(z_, q), dkv_all).astype(BF)
    for k in range(3):
        wait_in(kin.at[k], k_recv.at[k])
    for k in range(3):
        got = ks[3, zz[k]].astype(F32)
        for n in range(3):
            got += kin[n, zz[k]].astype(F32)
        kzs[k] = got.astype(BF)
        remote(kzs.at[k], kzin.at[k], kz_send.at[k], kz_recv.at[k], peer(q, r, zz[k])).start()

    for k in range(3):
        wait_in(zin.at[k], z_recv.at[k])
    for k in range(3):
        got = zs[3, qs[k]].astype(F32)
        for n in range(3):
            got += zin[n, qs[k]].astype(F32)
        qs_[k] = got.astype(BF)
        remote(qs_.at[k], qin.at[k], dq_send.at[k], dq_recv.at[k], peer(qs[k], r, z)).start()
    own_q = zs[3, q].astype(F32)
    own_k = ks[3, z].astype(F32)
    for n in range(3):
        own_q += zin[n, q].astype(F32)
        own_k += kin[n, z].astype(F32)
    for k in range(3):
        wait_in(qin.at[k], dq_recv.at[k])
        wait_in(kzin.at[k], kz_recv.at[k])
    for k in range(3):
        own_q += qin[k].astype(F32)
        own_k += kzin[k].astype(F32)
    fs[:, :, :, 0:QW] = own_q.astype(BF).reshape(RING, 2, 16, QW)
    fs[:, :, :, QW:GW] = own_k.astype(BF).reshape(RING, 2, 16, KV)

    for k in range(RING):
        to = turn(r, k)
        if k:
            remote(fs.at[to, c], fin.at[0, k], f_send.at[k], f_recv.at[k], (shard_of(c, q, to), z * 2 + c)).start()
        remote(fs.at[to, 1 - c], fin.at[1, k], f_send.at[RING + k], f_recv.at[RING + k],
               (shard_of(c, q, to), z * 2 + 1 - c)).start()
    fin[0, 0] = fs[r, c]
    for k in range(RING):
        if k:
            wait_in(fin.at[0, k], f_recv.at[k])
        wait_in(fin.at[1, k], f_recv.at[RING + k])
    for g in range(RING):
        mine = fin[0, lax.rem(r + RING - g, RING)].astype(F32)
        other = fin[1, lax.rem(q + RING - g, RING)].astype(F32)
        got = mine + other
        dw_out[:, g * QW:(g + 1) * QW] = got[:, 0:QW]
        dw_out[:, 2048 + g * HD:2048 + (g + 1) * HD] = got[:, QW:QW + HD]
        dw_out[:, 2560 + g * HD:2560 + (g + 1) * HD] = got[:, QW + HD:GW]

    for k in range(3):
        wait_in(att_out.at[:, pl.ds(pl.multiple_of(r_from[k] * QW, QW), QW)], att_recv.at[k])
    for copy in sent:
        copy.wait_send()
    own_att.wait()


def body(inputs, w_qkv, random_blocks, d_out):
    dma = pltpu.SemaphoreType.DMA
    vm = pltpu.VMEM
    hbm = pl.BlockSpec(memory_space=pl.ANY)
    attended, d_wqkv = pl.pallas_call(
        kernel,
        out_shape=[jax.ShapeDtypeStruct((TOK, D), BF), jax.ShapeDtypeStruct((16, RING * GW), F32)],
        in_specs=[pl.BlockSpec(memory_space=pltpu.SMEM), hbm, hbm, hbm],
        out_specs=[hbm, pl.BlockSpec(memory_space=pltpu.VMEM)],
        scratch_shapes=[
            vm((RING, TOK, D), BF),
            vm((D, RING * KV), BF),
            vm((RING, D, QW), BF),
            vm((RING, 2, BLOCK, KV), BF),
            vm((3, TOK, QW), BF),
            vm((QBLOCKS, BLOCK, KV), BF),
            vm((RING, TOK, QW), BF),
            vm((RING, TOK, QW), BF),
            vm((RING, TOK, QW), BF),
            vm((RING, TOK, QW), BF),
            vm((QBLOCKS, BLOCK, KV), F32),
            vm((PICKS + 1, BLOCK, KV), F32),
            vm((8 * BLOCK, KV), BF),
            pltpu.SMEM((PICKS,), jnp.int32),
            pltpu.SMEM((PICKS,), jnp.int32),
            pltpu.SMEM((QBLOCKS,), jnp.int32),
            vm((RING * RING, RING, 32, RING * TOK), BF),
            vm((QBLOCKS, BLOCK, KV), BF),
            vm((3, LOCAL, BLOCK, KV), BF),
            vm((LOCAL, BLOCK, KV), BF),
            vm((4, RING, 128, QW), BF),
            vm((3, RING, 128, QW), BF),
            vm((3, 128, QW), BF),
            vm((3, 128, QW), BF),
            vm((4, RING, 128, KV), BF),
            vm((3, RING, 128, KV), BF),
            vm((3, 128, KV), BF),
            vm((3, 128, KV), BF),
            vm((RING, 2, 16, GW), BF),
            vm((2, RING, 16, GW), BF),
            dma((4,)), dma((4,)),
            dma((3,)), dma((3,)), dma((12,)), dma((12,)), dma((3,)), dma((3,)), dma((3,)), dma((3,)), dma((6,)), dma((6,)),
            dma((3,)), dma((3,)), dma((3,)), dma((3,)), dma((3,)), dma((3,)), dma((3,)), dma((3,)), dma((3,)), dma((3,)),
            dma((3,)), dma((3,)), dma((8,)), dma((8,)),
        ],
        compiler_params=pltpu.CompilerParams(collective_id=1, has_side_effects=True, vmem_limit_bytes=62 * 2**20),
        cost_estimate=pl.CostEstimate(flops=13 * 10**9, bytes_accessed=20 * 2**20, transcendentals=2**22),
        name="attention_weight_gradient",
    )(random_blocks, inputs[0], w_qkv, d_out[0])
    return attended[None], d_wqkv


def solution(mesh):
    return jax.shard_map(
        body,
        mesh=mesh,
        in_specs=(P("dp", "seq", None), P(), P(), P("dp", "seq", None)),
        out_specs=(P("dp", "seq", None), P(("seq", "dp"), None)),
        check_vma=False,
    )
```

time: 679 us -> 106 us (0.16)
  waiting for transfers between devices: 397 us -> 0 us
  matrix products: 114 us -> 0 us
  Pallas kernels: 0 us -> 99.7 us
  local copies, waits for them, and re-layouts: 97 us -> 5.29 us
  other arithmetic: 44.8 us -> 0 us
  between operations: 14.3 us -> 0.64 us
  starting transfers between devices: 8.42 us -> 0 us
    unnamed x8 -> x0, waiting for transfers between devices: 125 us -> none
    psum x2 -> x0, waiting for transfers between devices: 117 us -> none  [the longest x1 76.8 us: broadcast(): return lax.psum(kept, axis)]
    pallas_call x0 -> x1, Pallas kernels: none -> 99.7 us  [body(): pl.pallas_call(kernel, out_shape=[jax.ShapeDtypeStruct((TOK, D), BF), jax...]
    dot_general x12 -> x0, matrix products: 99.2 us -> none  [the longest x2 27.5 us: attend(): jnp.einsum('grqk,kgd->qgrd', dweights, keys, preferred_element_type=jnp.f...]
    reduce_scatter x1 -> x0, waiting for transfers between devices: 88 us -> none  [body(): lax.psum_scatter(spread.astype(jnp.bfloat16), 'seq', scatter_dimension=1,...]
    all_gather x1 -> x0, waiting for transfers between devices: 55.9 us -> none  [body(): piece = lax.all_gather(kv_local, 'seq', axis=1, tiled=True)]
    dynamic_update_slice x10 -> x0, local copies, waits for them, and re-layouts: 23.5 us -> none  [body(): lax.map(attend_triple, (query_blocks, picked, grad_blocks))]
    dynamic_slice x13 -> x0, local copies, waits for them, and re-layouts: 19.1 us -> none  [the longest x12 19 us: body(): lax.map(attend_triple, (query_blocks, picked, grad_blocks))]
  transfers between devices with their start and end apart: 10 -> 0, of which waited for: 9 -> 0; matrix products, arithmetic and copies ran while one was open for 8% -> 0% of each run, Pallas kernels for 0% -> 0%
where the time goes in v2:
time: 106 us
  Pallas kernels  99.7 us (94%)
  local copies, waits for them, and re-layouts  5.29 us (5%)
    pallas_call x1, Pallas kernels, body(): pl.pallas_call(kernel, out_shape=[jax.ShapeDtypeStruct((TOK, D), BF), jax...  99.7 us
    unnamed x3, local copies, waits for them, and re-layouts  5.29 us

profile of v2, /device:TPU:1, one launch (start us, length us, event | category | flops | bytes accessed | tf_op | source)
XLA Modules:
  0.0 105.6 jit_solution(1297220444755585313)
XLA Ops:
  0.6 1.4 %copy.6.rb = s32[32,3]{1,0:T(8,128)} copy(s32[32,3]{0,1:T(4,128)} %param.6) | data formatting | bytes 768 | tf_op args[2]
  2.0 99.7 %attention_weight_gradient.1 = (bf16[256,2048]{1,0:T(8,128)(2,1)}, f32[16,3072]{1,0:T(8,128)}) custom-call(s32[32,3]{1,0:T(8,128)} %copy.6.rb, bf16[256,2048]{1,0:T(8,128)(2,1)} %bitcast.4, bf16[2048,3072]{1,0:T(8,128)(2,1)} %w_ref.1, bf16[256,2048]{1,0:T(8,128)(2,1)} %bitcast.5), custom_call_target="tpu_custom_call" | custom-call | flops 12999999488 | bytes 20971520 | tf_op jit(solution)/shard_map/attention_weight_gradient/pallas_call | solution.py:367
  101.7 2.3 %copy.9 = bf16[1,256,2048]{2,1,0:T(8,128)(2,1)} copy(bf16[1,256,2048]{2,1,0:T(8,128)(2,1)} %bitcast.3) | data formatting | bytes 2097152
  104.0 1.6 %copy.10 = f32[16,3072]{1,0:T(8,128)} copy(f32[16,3072]{1,0:T(8,128)} %get-tuple-element.9) | data formatting | bytes 393216

commit v3 on v2

--- a/solution.py
+++ b/solution.py
@@ -47,9 +47,9 @@
     return jnp.dot(a, b, preferred_element_type=F32)
 
 
-def kernel(rb, x_ref, w_ref, g_ref, att_out, dw_out,
+def kernel(rb, x_ref, w_ref, g_ref, att_out, fin_out,
            xall, wkv, wq, kvown, qown, kvall, qall, gall, attb, dqb, near, terms, kcat, ids, prev, last,
-           xt, dkvs, dkv_in, dkv, zs, zin, qs_, qin, ks, kin, kzs, kzin, fs, fin,
+           xt, dkvs, dkv_far, dkv_in, dkv, zs, z_far, zin, qs_, qin, ks, kin, kzs, kzin, fs, fin,
            local_sem, wq_sem, a_send, a_recv, kv_send, kv_recv, q_send, q_recv, g_send, g_recv, x_send, x_recv,
            dkv_send, dkv_recv, att_send, att_recv, z_send, z_recv, dq_send, dq_recv, k_send, k_recv, kz_send, kz_recv,
            f_send, f_recv):
@@ -108,13 +108,17 @@
         remote(kvown.at[rs[k]], slot(r), a_send.at[k], a_recv.at[k], peer(q, rs[k], z)).start()
 
     def pass_on(step, src, j):
-        for k in range(3):
-            remote(src, slot(j), kv_send.at[step * 3 + k], kv_recv.at[step * 3 + k], peer(qs[k], r, z)).start()
-
-    pass_on(0, kvown.at[r], r)
-    kvall[pl.ds((q * RING + r) * 2, 2)] = kvown[r]
-
-    for k in range(4):
+        for k in range(2):
+            remote(src, slot(j), kv_send.at[step * 4 + k], kv_recv.at[step * 4 + k], peer(qs[k], r, z)).start()
+
+    def pass_on_block(step, j):
+        for k in range(2):
+            whole = kvall.at[pl.ds((q_from[k] * RING + j) * 2, 2)]
+            wait_in(whole, kv_recv.at[step * 4 + k])
+            block = kvall.at[pl.ds((q_from[k] * RING + j) * 2 + k, 1)]
+            remote(block, block, kv_send.at[step * 4 + 2 + k], kv_recv.at[step * 4 + 2 + k], peer(qs[k], r, z)).start()
+
+    def project_queries(k):
         load_wq[k].wait()
         for part in range(2):
             cols = slice(part * 256, (part + 1) * 256)
@@ -124,9 +128,18 @@
             else:
                 qall[r, :, cols] = got
 
-    for k, j in enumerate(r_from):
-        wait_in(slot(j), a_recv.at[k])
-        pass_on(k + 1, slot(j), j)
+    pass_on(0, kvown.at[r], r)
+    kvall[pl.ds((q * RING + r) * 2, 2)] = kvown[r]
+    project_queries(0)
+    for k in range(2):
+        wait_in(slot(r_from[k]), a_recv.at[k])
+        pass_on(k + 1, slot(r_from[k]), r_from[k])
+    project_queries(1)
+    wait_in(slot(far), a_recv.at[2])
+    pass_on(3, slot(far), far)
+    pass_on_block(0, r)
+    project_queries(2)
+    project_queries(3)
 
     def step_j(step):
         return turn(r, jnp.where(step == 0, 0, jnp.where(step == 1, 3, step - 1)))
@@ -161,6 +174,9 @@
         return 0
 
     lax.fori_loop(0, QBLOCKS, fill_last, 0)
+    pass_on_block(1, down)
+    pass_on_block(2, up)
+    pass_on_block(3, far)
     near[...] = jnp.zeros_like(near)
     terms[PICKS] = jnp.zeros((BLOCK, KV), F32)
 
@@ -182,8 +198,8 @@
             remote(xall.at[up, halves[1]], xall.at[up, halves[1]], x_send.at[5], x_recv.at[5], peer(q, down, z))]
 
     for step, j in enumerate((r, down, up, far)):
-        for k in range(3):
-            wait_in(kvall.at[pl.ds((q_from[k] * RING + j) * 2, 2)], kv_recv.at[step * 3 + k])
+        for k in range(2):
+            wait_in(kvall.at[pl.ds((qs[2] * RING + j) * 2 + k, 1)], kv_recv.at[step * 4 + 2 + k])
     load_g.wait()
     for k in range(3):
         q_copies[k].start()
@@ -192,8 +208,13 @@
     def attend(i, _):
         @pl.when(i == 1)
         def _():
-            for copy in x_copies:
-                copy.start()
+            x_copies[0].start()
+            x_copies[1].start()
+
+        @pl.when(i == 3)
+        def _():
+            x_copies[2].start()
+            x_copies[3].start()
 
         for k in range(3):
             @pl.when(i == 2 * k + 2)
@@ -201,7 +222,7 @@
                 wait_in(qall.at[r_from[k]], q_recv.at[k])
                 wait_in(gall.at[r_from[k]], g_recv.at[k])
 
-        @pl.when(i == 7)
+        @pl.when(i == 6)
         def _():
             wait_in(xall.at[down, halves[0]], x_recv.at[0])
             x_on[0].start()
@@ -229,12 +250,12 @@
         dprob = lax.dot_general(values, grads, nt, preferred_element_type=F32)
         attended = dot(values.T, weights)
         mean = jnp.sum(probs * dprob, axis=0, keepdims=True)
-        dweights = (probs * (dprob - mean) * SCALE).astype(BF)
-        d_query = dot(keys.T, dweights)
+        dweights = (probs * (dprob - mean)).astype(BF)
+        d_query = dot(keys.T, dweights) * SCALE
         for h in heads:
             attb[j, rows, h] = attended[:, h].T.astype(BF)
             dqb[j, rows, h] = d_query[:, h].T.astype(BF)
-        d_key = dot(dweights, queries)
+        d_key = dot(dweights, queries) * SCALE
         d_value = dot(weights, grads)
         for l, n in enumerate(near_ids):
             at = slice(l * BLOCK, (l + 1) * BLOCK)
@@ -250,20 +271,53 @@
 
     lax.fori_loop(0, LOCAL, attend, 0)
 
-    for k in range(3):
-        def gather_terms(n, _):
+    def ring_far(chunk, landed, send, recv, to):
+        for k in range(2):
+            remote(chunk(2, k), landed.at[k], send.at[k], recv.at[k], to[k]).start()
+
+    def ring_free(chunk, arrived, send, recv, to):
+        for k in range(2):
+            remote(chunk(k, 1 - k), arrived(k, 1 - k), send.at[2 + k], recv.at[2 + k], to[k]).start()
+
+    def ring_rest(chunk, landed, arrived, send, recv, to):
+        for k in range(2):
+            wait_in(landed.at[k], recv.at[k])
+            chunk(k, k)[...] = (chunk(k, k)[...].astype(F32) + landed[k].astype(F32)).astype(BF)
+            remote(chunk(k, k), arrived(k, k), send.at[4 + k], recv.at[4 + k], to[k]).start()
+
+    def ring_wait(arrived, recv):
+        for k in range(2):
+            wait_in(arrived(k, 1 - k), recv.at[2 + k])
+            wait_in(arrived(k, k), recv.at[4 + k])
+
+    def dkv_chunk(k, half):
+        return dkvs.at[pl.ds(qs[k] * LOCAL + half * RING, RING)]
+
+    def dkv_arrived(k, half):
+        return dkv_in.at[k, pl.ds(half * RING, RING)]
+
+    q_peers = [peer(qs[k], r, z) for k in range(2)]
+    z_peers = [peer(q, r, zz[k]) for k in range(2)]
+
+    def gather_terms(k):
+        def one(n, _):
             at = qs[k] * LOCAL + n
             dkvs[at] = (near[at] + terms[last[at]]).astype(BF)
             return 0
 
-        lax.fori_loop(0, LOCAL, gather_terms, 0)
-        remote(dkvs.at[pl.ds(qs[k] * LOCAL, LOCAL)], dkv_in.at[k], dkv_send.at[k], dkv_recv.at[k],
-               peer(qs[k], r, z)).start()
+        lax.fori_loop(0, LOCAL, one, 0)
+
+    gather_terms(2)
+    ring_far(dkv_chunk, dkv_far, dkv_send, dkv_recv, q_peers)
+    gather_terms(0)
+    gather_terms(1)
+    ring_free(dkv_chunk, dkv_arrived, dkv_send, dkv_recv, q_peers)
 
     wait_in(xall.at[down, halves[1]], x_recv.at[2])
     transpose(down)
     wait_in(xall.at[up, halves[0]], x_recv.at[3])
     transpose(up)
+    ring_rest(dkv_chunk, dkv_far, dkv_arrived, dkv_send, dkv_recv, q_peers)
     wait_in(xall.at[far, halves[0]], x_recv.at[4])
     wait_in(xall.at[far, halves[1]], x_recv.at[5])
     transpose(far)
@@ -272,34 +326,44 @@
     def rows_of(z_, q_):
         return jnp.concatenate([xt[shard_of(c, q_, n), z_] for n in range(RING)], axis=0)
 
-    for k in (2, 0, 1):
+    def z_chunk(k, half):
+        return zs.at[k, pl.ds(half * 2, 2)]
+
+    def z_arrived(k, half):
+        return zin.at[k, pl.ds(half * 2, 2)]
+
+    def z_product(k, z_):
         for q_ in range(RING):
-            zs[k, q_] = dot(rows_of(zz[k], q_), dq_all).astype(BF)
-        remote(zs.at[k], zin.at[k], z_send.at[k], z_recv.at[k], peer(q, r, zz[k])).start()
-    for q_ in range(RING):
-        zs[3, q_] = dot(rows_of(z, q_), dq_all).astype(BF)
-
-    for k in range(3):
-        wait_in(dkv_in.at[k], dkv_recv.at[k])
+            zs[k, q_] = dot(rows_of(z_, q_), dq_all).astype(BF)
+
+    z_product(2, zz[2])
+    ring_far(z_chunk, z_far, z_send, z_recv, z_peers)
+    z_product(0, zz[0])
+    z_product(1, zz[1])
+    ring_free(z_chunk, z_arrived, z_send, z_recv, z_peers)
+    z_product(3, z)
+
+    ring_wait(dkv_arrived, dkv_recv)
 
     def add_terms(n, _):
         at = q * LOCAL + n
         got = near[at] + terms[last[at]]
-        for k in range(3):
+        for k in range(2):
             got += dkv_in[k, n].astype(F32)
         dkv[n] = got.astype(BF)
         return 0
 
     lax.fori_loop(0, LOCAL, add_terms, 0)
+    ring_rest(z_chunk, z_far, z_arrived, z_send, z_recv, z_peers)
     dkv_all = dkv[...].reshape(RING * TOK, KV)
     for k in (2, 0, 1):
         for z_ in range(RING):
             ks[k, z_] = dot(rows_of(z_, qs[k]), dkv_all).astype(BF)
         remote(ks.at[k], kin.at[k], k_send.at[k], k_recv.at[k], peer(qs[k], r, z)).start()
     for k in range(3):
-        remote(attb.at[rs[k]], att_out.at[:, pl.ds(pl.multiple_of(r * QW, QW), QW)],
+        remote(attb.at[rs[k]], att_out.at[r],
                att_send.at[k], att_recv.at[k], peer(q, rs[k], z)).start()
-    own_att = pltpu.make_async_copy(attb.at[r], att_out.at[:, pl.ds(pl.multiple_of(r * QW, QW), QW)], local_sem.at[3])
+    own_att = pltpu.make_async_copy(attb.at[r], att_out.at[r], local_sem.at[3])
     own_att.start()
     for z_ in range(RING):
         ks[3, z_] = dot(rows_of(z_, q), dkv_all).astype(BF)
@@ -312,19 +376,19 @@
         kzs[k] = got.astype(BF)
         remote(kzs.at[k], kzin.at[k], kz_send.at[k], kz_recv.at[k], peer(q, r, zz[k])).start()
 
-    for k in range(3):
-        wait_in(zin.at[k], z_recv.at[k])
+    ring_wait(z_arrived, z_recv)
     for k in range(3):
         got = zs[3, qs[k]].astype(F32)
-        for n in range(3):
+        for n in range(2):
             got += zin[n, qs[k]].astype(F32)
         qs_[k] = got.astype(BF)
         remote(qs_.at[k], qin.at[k], dq_send.at[k], dq_recv.at[k], peer(qs[k], r, z)).start()
     own_q = zs[3, q].astype(F32)
     own_k = ks[3, z].astype(F32)
     for n in range(3):
+        own_k += kin[n, z].astype(F32)
+    for n in range(2):
         own_q += zin[n, q].astype(F32)
-        own_k += kin[n, z].astype(F32)
     for k in range(3):
         wait_in(qin.at[k], dq_recv.at[k])
         wait_in(kzin.at[k], kz_recv.at[k])
@@ -346,27 +410,36 @@
             wait_in(fin.at[0, k], f_recv.at[k])
         wait_in(fin.at[1, k], f_recv.at[RING + k])
     for g in range(RING):
-        mine = fin[0, lax.rem(r + RING - g, RING)].astype(F32)
-        other = fin[1, lax.rem(q + RING - g, RING)].astype(F32)
-        got = mine + other
+        fin_out[0, g] = fin[0, lax.rem(r + RING - g, RING)]
+        fin_out[1, g] = fin[1, lax.rem(q + RING - g, RING)]
+
+    for k in range(3):
+        wait_in(att_out.at[r_from[k]], att_recv.at[k])
+    for copy in sent:
+        copy.wait_send()
+    own_att.wait()
+
+
+def results_kernel(att_ref, sums_ref, att_out, dw_out, sem):
+    copies = [pltpu.make_async_copy(att_ref.at[g], att_out.at[:, pl.ds(g * QW, QW)], sem.at[g]) for g in range(RING)]
+    for copy in copies:
+        copy.start()
+    for g in range(RING):
+        got = sums_ref[0, g].astype(F32) + sums_ref[1, g].astype(F32)
         dw_out[:, g * QW:(g + 1) * QW] = got[:, 0:QW]
         dw_out[:, 2048 + g * HD:2048 + (g + 1) * HD] = got[:, QW:QW + HD]
         dw_out[:, 2560 + g * HD:2560 + (g + 1) * HD] = got[:, QW + HD:GW]
-
-    for k in range(3):
-        wait_in(att_out.at[:, pl.ds(pl.multiple_of(r_from[k] * QW, QW), QW)], att_recv.at[k])
-    for copy in sent:
-        copy.wait_send()
-    own_att.wait()
+    for copy in copies:
+        copy.wait()
 
 
 def body(inputs, w_qkv, random_blocks, d_out):
     dma = pltpu.SemaphoreType.DMA
     vm = pltpu.VMEM
     hbm = pl.BlockSpec(memory_space=pl.ANY)
-    attended, d_wqkv = pl.pallas_call(
+    attended, sums = pl.pallas_call(
         kernel,
-        out_shape=[jax.ShapeDtypeStruct((TOK, D), BF), jax.ShapeDtypeStruct((16, RING * GW), F32)],
+        out_shape=[jax.ShapeDtypeStruct((RING, TOK, QW), BF), jax.ShapeDtypeStruct((2, RING, 16, GW), BF)],
         in_specs=[pl.BlockSpec(memory_space=pltpu.SMEM), hbm, hbm, hbm],
         out_specs=[hbm, pl.BlockSpec(memory_space=pltpu.VMEM)],
         scratch_shapes=[
@@ -388,10 +461,12 @@
             pltpu.SMEM((QBLOCKS,), jnp.int32),
             vm((RING * RING, RING, 32, RING * TOK), BF),
             vm((QBLOCKS, BLOCK, KV), BF),
-            vm((3, LOCAL, BLOCK, KV), BF),
+            vm((2, RING, BLOCK, KV), BF),
+            vm((2, LOCAL, BLOCK, KV), BF),
             vm((LOCAL, BLOCK, KV), BF),
             vm((4, RING, 128, QW), BF),
-            vm((3, RING, 128, QW), BF),
+            vm((2, 2, 128, QW), BF),
+            vm((2, RING, 128, QW), BF),
             vm((3, 128, QW), BF),
             vm((3, 128, QW), BF),
             vm((4, RING, 128, KV), BF),
@@ -401,14 +476,22 @@
             vm((RING, 2, 16, GW), BF),
             vm((2, RING, 16, GW), BF),
             dma((4,)), dma((4,)),
-            dma((3,)), dma((3,)), dma((12,)), dma((12,)), dma((3,)), dma((3,)), dma((3,)), dma((3,)), dma((6,)), dma((6,)),
-            dma((3,)), dma((3,)), dma((3,)), dma((3,)), dma((3,)), dma((3,)), dma((3,)), dma((3,)), dma((3,)), dma((3,)),
+            dma((3,)), dma((3,)), dma((16,)), dma((16,)), dma((3,)), dma((3,)), dma((3,)), dma((3,)), dma((6,)), dma((6,)),
+            dma((6,)), dma((6,)), dma((3,)), dma((3,)), dma((6,)), dma((6,)), dma((3,)), dma((3,)), dma((3,)), dma((3,)),
             dma((3,)), dma((3,)), dma((8,)), dma((8,)),
         ],
         compiler_params=pltpu.CompilerParams(collective_id=1, has_side_effects=True, vmem_limit_bytes=62 * 2**20),
         cost_estimate=pl.CostEstimate(flops=13 * 10**9, bytes_accessed=20 * 2**20, transcendentals=2**22),
         name="attention_weight_gradient",
     )(random_blocks, inputs[0], w_qkv, d_out[0])
+    attended, d_wqkv = pl.pallas_call(
+        results_kernel,
+        out_shape=[jax.ShapeDtypeStruct((TOK, D), BF), jax.ShapeDtypeStruct((16, RING * GW), F32)],
+        in_specs=[hbm, pl.BlockSpec(memory_space=pltpu.VMEM)],
+        out_specs=[hbm, pl.BlockSpec(memory_space=pltpu.VMEM)],
+        scratch_shapes=[dma((RING,))],
+        name="results",
+    )(attended, sums)
     return attended[None], d_wqkv
 
 

time: 106 us -> 132 us (1.25)
  Pallas kernels: 99.7 us -> 130 us
  local copies, waits for them, and re-layouts: 5.29 us -> 1.37 us
    pallas_call x1 -> x2, Pallas kernels: 99.7 us -> 130 us  [the longest x1 95.5 us: body(): pl.pallas_call(kernel, out_shape=[jax.ShapeDtypeStruct((RING, TOK, QW), B...]
    unnamed x3 -> x1, local copies, waits for them, and re-layouts: 5.29 us -> 1.37 us
where the time goes in v3:
time: 132 us
  Pallas kernels  130 us (98%)
  local copies, waits for them, and re-layouts  1.37 us (1%)
    pallas_call x1, Pallas kernels, body(): pl.pallas_call(kernel, out_shape=[jax.ShapeDtypeStruct((RING, TOK, QW), B...  95.5 us
    pallas_call x1, Pallas kernels, body(): pl.pallas_call(results_kernel, out_shape=[jax.ShapeDtypeStruct((TOK, D),...  34.5 us

profile of v3, /device:TPU:1, one launch (start us, length us, event | category | flops | bytes accessed | tf_op | source)
XLA Modules:
  0.0 132.0 jit_solution(5346720725413922234)
XLA Ops:
  0.6 1.4 %copy.6.rb = s32[32,3]{1,0:T(8,128)} copy(s32[32,3]{0,1:T(4,128)} %param.6) | data formatting | bytes 768 | tf_op args[2]
  2.0 95.5 %attention_weight_gradient.1 = (bf16[4,256,512]{2,1,0:T(8,128)(2,1)}, bf16[2,4,16,768]{3,2,1,0:T(8,128)(2,1)}) custom-call(s32[32,3]{1,0:T(8,128)} %copy.6.rb, bf16[256,2048]{1,0:T(8,128)(2,1)} %bitcast.3, bf16[2048,3072]{1,0:T(8,128)(2,1)} %w_ref.1, bf16[256,2048]{1,0:T(8,128)(2,1)} %bitcast.4), custom_call_target="tpu_custom_call" | custom-call | flops 12999999488 | bytes 20971520 | tf_op jit(solution)/shard_map/attention_weight_gradient/pallas_call | solution.py:440
  97.5 34.5 %results.1 = (bf16[256,2048]{1,0:T(8,128)(2,1)}, f32[16,3072]{1,0:T(8,128)}) custom-call(bf16[4,256,512]{2,1,0:T(8,128)(2,1)} %get-tuple-element.6.att_ref, bf16[2,4,16,768]{3,2,1,0:T(8,128)(2,1)} %get-tuple-element.7.sums_ref), custom_call_target="tpu_custom_call" | custom-call | tf_op jit(solution)/shard_map/results/pallas_call | solution.py:487

commit v4 on v3

--- a/solution.py
+++ b/solution.py
@@ -48,9 +48,9 @@
 
 
 def kernel(rb, x_ref, w_ref, g_ref, att_out, fin_out,
-           xall, wkv, wq, kvown, qown, kvall, qall, gall, attb, dqb, near, terms, kcat, ids, prev, last,
+           xown, wkv, wq, gown, kvown, qown, kvall, qall, gall, attb, dqb, near, terms, kcat, last,
            xt, dkvs, dkv_far, dkv_in, dkv, zs, z_far, zin, qs_, qin, ks, kin, kzs, kzin, fs, fin,
-           local_sem, wq_sem, a_send, a_recv, kv_send, kv_recv, q_send, q_recv, g_send, g_recv, x_send, x_recv,
+           local_sem, wq_sem, g_sem, a_send, a_recv, kv_send, kv_recv, q_send, q_recv, g_send, g_recv, x_send, x_recv,
            dkv_send, dkv_recv, att_send, att_recv, z_send, z_recv, dq_send, dq_recv, k_send, k_recv, kz_send, kz_recv,
            f_send, f_recv):
     q, r, z, c = places()
@@ -64,11 +64,12 @@
     def peer(q_, r_, z_):
         return (shard_of(c, q_, r_), z_ * 2 + c)
 
-    load_x = pltpu.make_async_copy(x_ref, xall.at[r], local_sem.at[0])
+    load_x = pltpu.make_async_copy(x_ref, xown, local_sem.at[0])
     load_x.start()
     load_wkv = pltpu.make_async_copy(w_ref.at[:, pl.ds(RING * QW, RING * KV)], wkv, local_sem.at[1])
     load_wkv.start()
-    load_g = pltpu.make_async_copy(g_ref.at[:, pl.ds(pl.multiple_of(r * QW, QW), QW)], gall.at[r], local_sem.at[2])
+    load_g = [pltpu.make_async_copy(g_ref.at[:, pl.ds(pl.multiple_of(to * QW, QW), QW)], dst, g_sem.at[k])
+              for k, (to, dst) in enumerate(((up, gown.at[0]), (down, gown.at[1]), (far, gown.at[2]), (r, gall.at[r])))]
     load_wq = [pltpu.make_async_copy(w_ref.at[:, pl.ds(pl.multiple_of(to * QW, QW), QW)], wq.at[k], wq_sem.at[k])
                for k, to in enumerate((up, down, far, r))]
 
@@ -88,17 +89,26 @@
         sent.append(copy)
         return copy
 
+    def step_j(step):
+        return turn(r, jnp.where(step == 0, 0, jnp.where(step == 1, 3, step - 1)))
+
+    def place_of(n):
+        s = n // 2
+        return (s + c * ((s % RING) * RING + s // RING - s)) * 2 + n % 2
+
     load_x.wait()
     load_wkv.wait()
     for copy in load_wq:
         copy.start()
-    load_g.start()
-    x_own = xall[r]
+    for copy in load_g:
+        copy.start()
+    x_own = xown[...]
     for part in range(4):
         got = dot(x_own, wkv[:, part * 256:(part + 1) * 256]).astype(BF)
         cols = slice(0, HD) if part < 2 else slice(HD, KV)
         for n in range(2):
             kvown[part % 2 * 2 + n, :, :, cols] = got[:, n * HD:(n + 1) * HD].reshape(2, BLOCK, HD)
+
     pl.semaphore_wait(barrier, len(met))
 
     def slot(j):
@@ -128,82 +138,44 @@
             else:
                 qall[r, :, cols] = got
 
+    q_copies = [remote(qown.at[k], qall.at[r], q_send.at[k], q_recv.at[k], peer(q, rs[k], z)) for k in range(3)]
+    g_copies = [remote(gown.at[k], gall.at[r], g_send.at[k], g_recv.at[k], peer(q, rs[k], z)) for k in range(3)]
+    halves = (pl.ds(0, 2 * RING), pl.ds(2 * RING, 2 * RING))
+    x_copies = [remote(xt.at[r, halves[half]], xt.at[r, halves[half]], x_send.at[n], x_recv.at[n], peer(q, to, z))
+                for n, (half, to) in enumerate(((0, up), (1, down), (1, up), (0, down)))]
+    x_on = [remote(xt.at[down, halves[0]], xt.at[down, halves[0]], x_send.at[4], x_recv.at[4], peer(q, up, z)),
+            remote(xt.at[up, halves[1]], xt.at[up, halves[1]], x_send.at[5], x_recv.at[5], peer(q, down, z))]
+
     pass_on(0, kvown.at[r], r)
     kvall[pl.ds((q * RING + r) * 2, 2)] = kvown[r]
-    project_queries(0)
+    for copy in load_g:
+        copy.wait()
+    for k in range(2):
+        g_copies[k].start()
+    xt[r] = x_own.T.reshape(RING * RING, RING, 32, TOK)
+    near[...] = jnp.zeros_like(near)
+    terms[PICKS] = jnp.zeros((BLOCK, KV), F32)
+    for n in range(QBLOCKS):
+        last[n] = PICKS
     for k in range(2):
         wait_in(slot(r_from[k]), a_recv.at[k])
         pass_on(k + 1, slot(r_from[k]), r_from[k])
-    project_queries(1)
+    project_queries(0)
     wait_in(slot(far), a_recv.at[2])
     pass_on(3, slot(far), far)
     pass_on_block(0, r)
-    project_queries(2)
-    project_queries(3)
-
-    def step_j(step):
-        return turn(r, jnp.where(step == 0, 0, jnp.where(step == 1, 3, step - 1)))
-
-    def place_of(n):
-        s = n // 2
-        return (s + c * ((s % RING) * RING + s // RING - s)) * 2 + n % 2
-
-    def fill_ids(i, _):
-        b = shard_of(c, q, step_j(i // 2)) * 2 + i % 2
-        for n in range(NRAND):
-            ids[i * NRAND + n] = place_of(rb[b, n])
-        return 0
-
-    lax.fori_loop(0, LOCAL, fill_ids, 0)
-
-    def fill_prev(k, _):
-        mine = ids[k]
-        got = jnp.int32(PICKS)
-        for n in range(PICKS):
-            got = jnp.where((ids[n] == mine) & (n < k), n, got)
-        prev[k] = got
-        return 0
-
-    lax.fori_loop(0, PICKS, fill_prev, 0)
-
-    def fill_last(n, _):
-        got = jnp.int32(PICKS)
-        for k in range(PICKS):
-            got = jnp.where(ids[k] == n, k, got)
-        last[n] = got
-        return 0
-
-    lax.fori_loop(0, QBLOCKS, fill_last, 0)
+    project_queries(1)
     pass_on_block(1, down)
     pass_on_block(2, up)
+    project_queries(2)
     pass_on_block(3, far)
-    near[...] = jnp.zeros_like(near)
-    terms[PICKS] = jnp.zeros((BLOCK, KV), F32)
-
-    def transpose(j):
-        turned = xall[j].T.reshape(RING * RING, RING, 32, TOK)
-        xt[:, :, :, pl.ds(pl.multiple_of(j * TOK, TOK), TOK)] = turned
-
-    transpose(r)
-
-    q_copies, g_copies = [], []
-    for k in range(3):
-        q_copies.append(remote(qown.at[k], qall.at[r], q_send.at[k], q_recv.at[k], peer(q, rs[k], z)))
-        g_copies.append(remote(g_ref.at[:, pl.ds(pl.multiple_of(rs[k] * QW, QW), QW)], gall.at[r],
-                               g_send.at[k], g_recv.at[k], peer(q, rs[k], z)))
-    halves = (pl.ds(0, BLOCK), pl.ds(BLOCK, BLOCK))
-    x_copies = [remote(xall.at[r, halves[half]], xall.at[r, halves[half]], x_send.at[n], x_recv.at[n], peer(q, to, z))
-                for n, (half, to) in enumerate(((0, up), (1, down), (1, up), (0, down)))]
-    x_on = [remote(xall.at[down, halves[0]], xall.at[down, halves[0]], x_send.at[4], x_recv.at[4], peer(q, up, z)),
-            remote(xall.at[up, halves[1]], xall.at[up, halves[1]], x_send.at[5], x_recv.at[5], peer(q, down, z))]
+    project_queries(3)
 
     for step, j in enumerate((r, down, up, far)):
         for k in range(2):
             wait_in(kvall.at[pl.ds((qs[2] * RING + j) * 2 + k, 1)], kv_recv.at[step * 4 + 2 + k])
-    load_g.wait()
-    for k in range(3):
+    for k in range(2):
         q_copies[k].start()
-        g_copies[k].start()
 
     def attend(i, _):
         @pl.when(i == 1)
@@ -211,10 +183,10 @@
             x_copies[0].start()
             x_copies[1].start()
 
-        @pl.when(i == 3)
+        @pl.when(i == 2)
         def _():
-            x_copies[2].start()
-            x_copies[3].start()
+            q_copies[2].start()
+            g_copies[2].start()
 
         for k in range(3):
             @pl.when(i == 2 * k + 2)
@@ -222,11 +194,16 @@
                 wait_in(qall.at[r_from[k]], q_recv.at[k])
                 wait_in(gall.at[r_from[k]], g_recv.at[k])
 
+        @pl.when(i == 3)
+        def _():
+            x_copies[2].start()
+            x_copies[3].start()
+
         @pl.when(i == 6)
         def _():
-            wait_in(xall.at[down, halves[0]], x_recv.at[0])
+            wait_in(xt.at[down, halves[0]], x_recv.at[0])
             x_on[0].start()
-            wait_in(xall.at[up, halves[1]], x_recv.at[1])
+            wait_in(xt.at[up, halves[1]], x_recv.at[1])
             x_on[1].start()
 
         j = step_j(i // 2)
@@ -234,7 +211,8 @@
         rows = pl.ds(pl.multiple_of((i % 2) * BLOCK, BLOCK), BLOCK)
         near_ids = [place_of(n) for n in (lax.rem(b + QBLOCKS - 1, QBLOCKS), b, lax.rem(b + 1, QBLOCKS),
                                           jnp.int32(0), jnp.int32(1))]
-        listed = near_ids + [ids[i * NRAND + n] for n in range(NRAND)]
+        far_ids = [place_of(rb[b, n]) for n in range(NRAND)]
+        listed = near_ids + far_ids
         for l, n in enumerate(listed):
             kcat[pl.ds(l * BLOCK, BLOCK), :] = kvall[n]
         keys, values = kcat[:, :HD], kcat[:, HD:]
@@ -263,10 +241,14 @@
             near[n, :, HD:] += d_value[at]
         for l in range(NRAND):
             at = slice((5 + l) * BLOCK, (6 + l) * BLOCK)
-            k = i * NRAND + l
-            before = terms[prev[k]]
-            terms[k, :, 0:HD] = before[:, 0:HD] + d_key[at]
-            terms[k, :, HD:] = before[:, HD:] + d_value[at]
+            before = terms[last[far_ids[l]]]
+            terms[i * NRAND + l, :, 0:HD] = before[:, 0:HD] + d_key[at]
+            terms[i * NRAND + l, :, HD:] = before[:, HD:] + d_value[at]
+        for n in range(QBLOCKS):
+            got = last[n]
+            for l in range(NRAND):
+                got = jnp.where(far_ids[l] == n, i * NRAND + l, got)
+            last[n] = got
         return 0
 
     lax.fori_loop(0, LOCAL, attend, 0)
@@ -308,23 +290,17 @@
         lax.fori_loop(0, LOCAL, one, 0)
 
     gather_terms(2)
-    ring_far(dkv_chunk, dkv_far, dkv_send, dkv_recv, q_peers)
     gather_terms(0)
     gather_terms(1)
-    ring_free(dkv_chunk, dkv_arrived, dkv_send, dkv_recv, q_peers)
-
-    wait_in(xall.at[down, halves[1]], x_recv.at[2])
-    transpose(down)
-    wait_in(xall.at[up, halves[0]], x_recv.at[3])
-    transpose(up)
-    ring_rest(dkv_chunk, dkv_far, dkv_arrived, dkv_send, dkv_recv, q_peers)
-    wait_in(xall.at[far, halves[0]], x_recv.at[4])
-    wait_in(xall.at[far, halves[1]], x_recv.at[5])
-    transpose(far)
+    wait_in(xt.at[down, halves[1]], x_recv.at[2])
+    wait_in(xt.at[up, halves[0]], x_recv.at[3])
+    wait_in(xt.at[far, halves[0]], x_recv.at[4])
+    wait_in(xt.at[far, halves[1]], x_recv.at[5])
     dq_all = dqb[...].reshape(RING * TOK, QW)
 
     def rows_of(z_, q_):
-        return jnp.concatenate([xt[shard_of(c, q_, n), z_] for n in range(RING)], axis=0)
+        return jnp.concatenate([jnp.concatenate([xt[j, shard_of(c, q_, n), z_] for n in range(RING)], axis=0)
+                                for j in range(RING)], axis=1)
 
     def z_chunk(k, half):
         return zs.at[k, pl.ds(half * 2, 2)]
@@ -333,14 +309,17 @@
         return zin.at[k, pl.ds(half * 2, 2)]
 
     def z_product(k, z_):
-        for q_ in range(RING):
-            zs[k, q_] = dot(rows_of(z_, q_), dq_all).astype(BF)
+        rows = jnp.concatenate([rows_of(z_, q_) for q_ in range(RING)], axis=0)
+        zs[k] = dot(rows, dq_all).astype(BF).reshape(RING, 128, QW)
 
     z_product(2, zz[2])
     ring_far(z_chunk, z_far, z_send, z_recv, z_peers)
+    ring_far(dkv_chunk, dkv_far, dkv_send, dkv_recv, q_peers)
+    ring_free(dkv_chunk, dkv_arrived, dkv_send, dkv_recv, q_peers)
     z_product(0, zz[0])
     z_product(1, zz[1])
     ring_free(z_chunk, z_arrived, z_send, z_recv, z_peers)
+    ring_rest(dkv_chunk, dkv_far, dkv_arrived, dkv_send, dkv_recv, q_peers)
     z_product(3, z)
 
     ring_wait(dkv_arrived, dkv_recv)
@@ -354,19 +333,17 @@
         return 0
 
     lax.fori_loop(0, LOCAL, add_terms, 0)
+    dkv_all = dkv[...].reshape(RING * TOK, KV)
+
+    def k_product(k, q_):
+        rows = jnp.concatenate([rows_of(z_, q_) for z_ in range(RING)], axis=0)
+        ks[k] = dot(rows, dkv_all).astype(BF).reshape(RING, 128, KV)
+
+    for k in (2, 0, 1):
+        k_product(k, qs[k])
+        remote(ks.at[k], kin.at[k], k_send.at[k], k_recv.at[k], peer(qs[k], r, z)).start()
+    k_product(3, q)
     ring_rest(z_chunk, z_far, z_arrived, z_send, z_recv, z_peers)
-    dkv_all = dkv[...].reshape(RING * TOK, KV)
-    for k in (2, 0, 1):
-        for z_ in range(RING):
-            ks[k, z_] = dot(rows_of(z_, qs[k]), dkv_all).astype(BF)
-        remote(ks.at[k], kin.at[k], k_send.at[k], k_recv.at[k], peer(qs[k], r, z)).start()
-    for k in range(3):
-        remote(attb.at[rs[k]], att_out.at[r],
-               att_send.at[k], att_recv.at[k], peer(q, rs[k], z)).start()
-    own_att = pltpu.make_async_copy(attb.at[r], att_out.at[r], local_sem.at[3])
-    own_att.start()
-    for z_ in range(RING):
-        ks[3, z_] = dot(rows_of(z_, q), dkv_all).astype(BF)
     for k in range(3):
         wait_in(kin.at[k], k_recv.at[k])
     for k in range(3):
@@ -376,6 +353,11 @@
         kzs[k] = got.astype(BF)
         remote(kzs.at[k], kzin.at[k], kz_send.at[k], kz_recv.at[k], peer(q, r, zz[k])).start()
 
+    for k in range(3):
+        remote(attb.at[rs[k]], att_out.at[r],
+               att_send.at[k], att_recv.at[k], peer(q, rs[k], z)).start()
+    own_att = pltpu.make_async_copy(attb.at[r], att_out.at[r], local_sem.at[3])
+    own_att.start()
     ring_wait(z_arrived, z_recv)
     for k in range(3):
         got = zs[3, qs[k]].astype(F32)
@@ -420,17 +402,13 @@
     own_att.wait()
 
 
-def results_kernel(att_ref, sums_ref, att_out, dw_out, sem):
-    copies = [pltpu.make_async_copy(att_ref.at[g], att_out.at[:, pl.ds(g * QW, QW)], sem.at[g]) for g in range(RING)]
-    for copy in copies:
-        copy.start()
+def results_kernel(att_ref, sums_ref, att_out, dw_out):
     for g in range(RING):
+        att_out[:, g * QW:(g + 1) * QW] = att_ref[g]
         got = sums_ref[0, g].astype(F32) + sums_ref[1, g].astype(F32)
         dw_out[:, g * QW:(g + 1) * QW] = got[:, 0:QW]
         dw_out[:, 2048 + g * HD:2048 + (g + 1) * HD] = got[:, QW:QW + HD]
         dw_out[:, 2560 + g * HD:2560 + (g + 1) * HD] = got[:, QW + HD:GW]
-    for copy in copies:
-        copy.wait()
 
 
 def body(inputs, w_qkv, random_blocks, d_out):
@@ -443,9 +421,10 @@
         in_specs=[pl.BlockSpec(memory_space=pltpu.SMEM), hbm, hbm, hbm],
         out_specs=[hbm, pl.BlockSpec(memory_space=pltpu.VMEM)],
         scratch_shapes=[
-            vm((RING, TOK, D), BF),
+            vm((TOK, D), BF),
             vm((D, RING * KV), BF),
             vm((RING, D, QW), BF),
+            vm((3, TOK, QW), BF),
             vm((RING, 2, BLOCK, KV), BF),
             vm((3, TOK, QW), BF),
             vm((QBLOCKS, BLOCK, KV), BF),
@@ -456,10 +435,8 @@
             vm((QBLOCKS, BLOCK, KV), F32),
             vm((PICKS + 1, BLOCK, KV), F32),
             vm((8 * BLOCK, KV), BF),
-            pltpu.SMEM((PICKS,), jnp.int32),
-            pltpu.SMEM((PICKS,), jnp.int32),
             pltpu.SMEM((QBLOCKS,), jnp.int32),
-            vm((RING * RING, RING, 32, RING * TOK), BF),
+            vm((RING, RING * RING, RING, 32, TOK), BF),
             vm((QBLOCKS, BLOCK, KV), BF),
             vm((2, RING, BLOCK, KV), BF),
             vm((2, LOCAL, BLOCK, KV), BF),
@@ -475,7 +452,7 @@
             vm((3, 128, KV), BF),
             vm((RING, 2, 16, GW), BF),
             vm((2, RING, 16, GW), BF),
-            dma((4,)), dma((4,)),
+            dma((4,)), dma((4,)), dma((4,)),
             dma((3,)), dma((3,)), dma((16,)), dma((16,)), dma((3,)), dma((3,)), dma((3,)), dma((3,)), dma((6,)), dma((6,)),
             dma((6,)), dma((6,)), dma((3,)), dma((3,)), dma((6,)), dma((6,)), dma((3,)), dma((3,)), dma((3,)), dma((3,)),
             dma((3,)), dma((3,)), dma((8,)), dma((8,)),
@@ -487,9 +464,8 @@
     attended, d_wqkv = pl.pallas_call(
         results_kernel,
         out_shape=[jax.ShapeDtypeStruct((TOK, D), BF), jax.ShapeDtypeStruct((16, RING * GW), F32)],
-        in_specs=[hbm, pl.BlockSpec(memory_space=pltpu.VMEM)],
-        out_specs=[hbm, pl.BlockSpec(memory_space=pltpu.VMEM)],
-        scratch_shapes=[dma((RING,))],
+        in_specs=[pl.BlockSpec(memory_space=pltpu.VMEM)] * 2,
+        out_specs=[pl.BlockSpec(memory_space=pltpu.VMEM)] * 2,
         name="results",
     )(attended, sums)
     return attended[None], d_wqkv

time: 132 us -> 95.6 us (0.72)
  Pallas kernels: 130 us -> 93.4 us
    pallas_call x1, Pallas kernels: 34.5 us -> 2.35 us  [body(): pl.pallas_call(results_kernel, out_shape=[jax.ShapeDtypeStruct((TOK, D),...]
    pallas_call x1, Pallas kernels: 95.5 us -> 91 us  [body(): pl.pallas_call(kernel, out_shape=[jax.ShapeDtypeStruct((RING, TOK, QW), B...]
where the time goes in v4:
time: 95.6 us; the launch traced here: 95.4 us
  Pallas kernels  93.4 us (98%)
  local copies, waits for them, and re-layouts  1.37 us (1%)
    pallas_call x1, Pallas kernels, body(): pl.pallas_call(kernel, out_shape=[jax.ShapeDtypeStruct((RING, TOK, QW), B...  91 us
    pallas_call x1, Pallas kernels, body(): pl.pallas_call(results_kernel, out_shape=[jax.ShapeDtypeStruct((TOK, D),...  2.35 us

profile of v4, /device:TPU:1, one launch (start us, length us, event | category | flops | bytes accessed | tf_op | source)
XLA Modules:
  0.0 95.4 jit_solution(16838101175822013786)
XLA Ops:
  0.6 1.4 %copy.6.rb = s32[32,3]{1,0:T(8,128)} copy(s32[32,3]{0,1:T(4,128)} %param.6) | data formatting | bytes 768 | tf_op args[2]
  2.0 91.0 %attention_weight_gradient.1 = (bf16[4,256,512]{2,1,0:T(8,128)(2,1)}, bf16[2,4,16,768]{3,2,1,0:T(8,128)(2,1)}) custom-call(s32[32,3]{1,0:T(8,128)} %copy.6.rb, bf16[256,2048]{1,0:T(8,128)(2,1)} %bitcast.3, bf16[2048,3072]{1,0:T(8,128)(2,1)} %w_ref.1, bf16[256,2048]{1,0:T(8,128)(2,1)} %bitcast.4), custom_call_target="tpu_custom_call" | custom-call | flops 12999999488 | bytes 20971520 | tf_op jit(solution)/shard_map/attention_weight_gradient/pallas_call | solution.py:418
  93.0 2.4 %results.1 = (bf16[256,2048]{1,0:T(8,128)(2,1)}, f32[16,3072]{1,0:T(8,128)}) custom-call(bf16[4,256,512]{2,1,0:T(8,128)(2,1)} %get-tuple-element.6.att_ref, bf16[2,4,16,768]{3,2,1,0:T(8,128)(2,1)} %get-tuple-element.7.sums_ref), custom_call_target="tpu_custom_call" | custom-call | tf_op jit(solution)/shard_map/results/pallas_call | solution.py:464

commit v5 on v4

--- a/solution.py
+++ b/solution.py
@@ -47,8 +47,8 @@
     return jnp.dot(a, b, preferred_element_type=F32)
 
 
-def kernel(rb, x_ref, w_ref, g_ref, att_out, fin_out,
-           xown, wkv, wq, gown, kvown, qown, kvall, qall, gall, attb, dqb, near, terms, kcat, last,
+def kernel(rb_ref, x_ref, w_ref, g_ref, att_out, fin_out,
+           rb, rb_sem, xown, wkv, wq, gown, kvown, qown, kvall, qall, gall, attb, dqb, near, terms, kcat, last,
            xt, dkvs, dkv_far, dkv_in, dkv, zs, z_far, zin, qs_, qin, ks, kin, kzs, kzin, fs, fin,
            local_sem, wq_sem, g_sem, a_send, a_recv, kv_send, kv_recv, q_send, q_recv, g_send, g_recv, x_send, x_recv,
            dkv_send, dkv_recv, att_send, att_recv, z_send, z_recv, dq_send, dq_recv, k_send, k_recv, kz_send, kz_recv,
@@ -65,6 +65,8 @@
         return (shard_of(c, q_, r_), z_ * 2 + c)
 
     load_x = pltpu.make_async_copy(x_ref, xown, local_sem.at[0])
+    load_rb = pltpu.make_async_copy(rb_ref, rb, rb_sem)
+    load_rb.start()
     load_x.start()
     load_wkv = pltpu.make_async_copy(w_ref.at[:, pl.ds(RING * QW, RING * KV)], wkv, local_sem.at[1])
     load_wkv.start()
@@ -96,6 +98,7 @@
         s = n // 2
         return (s + c * ((s % RING) * RING + s // RING - s)) * 2 + n % 2
 
+    load_rb.wait()
     load_x.wait()
     load_wkv.wait()
     for copy in load_wq:
@@ -174,15 +177,12 @@
     for step, j in enumerate((r, down, up, far)):
         for k in range(2):
             wait_in(kvall.at[pl.ds((qs[2] * RING + j) * 2 + k, 1)], kv_recv.at[step * 4 + 2 + k])
+    x_copies[0].start()
+    x_copies[1].start()
     for k in range(2):
         q_copies[k].start()
 
     def attend(i, _):
-        @pl.when(i == 1)
-        def _():
-            x_copies[0].start()
-            x_copies[1].start()
-
         @pl.when(i == 2)
         def _():
             q_copies[2].start()
@@ -194,12 +194,12 @@
                 wait_in(qall.at[r_from[k]], q_recv.at[k])
                 wait_in(gall.at[r_from[k]], g_recv.at[k])
 
-        @pl.when(i == 3)
+        @pl.when(i == 1)
         def _():
             x_copies[2].start()
             x_copies[3].start()
 
-        @pl.when(i == 6)
+        @pl.when(i == 5)
         def _():
             wait_in(xt.at[down, halves[0]], x_recv.at[0])
             x_on[0].start()
@@ -211,7 +211,7 @@
         rows = pl.ds(pl.multiple_of((i % 2) * BLOCK, BLOCK), BLOCK)
         near_ids = [place_of(n) for n in (lax.rem(b + QBLOCKS - 1, QBLOCKS), b, lax.rem(b + 1, QBLOCKS),
                                           jnp.int32(0), jnp.int32(1))]
-        far_ids = [place_of(rb[b, n]) for n in range(NRAND)]
+        far_ids = [place_of(rb[n, b]) for n in range(NRAND)]
         listed = near_ids + far_ids
         for l, n in enumerate(listed):
             kcat[pl.ds(l * BLOCK, BLOCK), :] = kvall[n]
@@ -414,13 +414,15 @@
 def body(inputs, w_qkv, random_blocks, d_out):
     dma = pltpu.SemaphoreType.DMA
     vm = pltpu.VMEM
-    hbm = pl.BlockSpec(memory_space=pl.ANY)
+    hbm = pl.BlockSpec(memory_space=pltpu.HBM)
     attended, sums = pl.pallas_call(
         kernel,
         out_shape=[jax.ShapeDtypeStruct((RING, TOK, QW), BF), jax.ShapeDtypeStruct((2, RING, 16, GW), BF)],
-        in_specs=[pl.BlockSpec(memory_space=pltpu.SMEM), hbm, hbm, hbm],
-        out_specs=[hbm, pl.BlockSpec(memory_space=pltpu.VMEM)],
+        in_specs=[hbm, hbm, hbm, hbm],
+        out_specs=[pl.BlockSpec(memory_space=pltpu.VMEM)] * 2,
         scratch_shapes=[
+            pltpu.SMEM((NRAND, QBLOCKS), jnp.int32),
+            dma(()),
             vm((TOK, D), BF),
             vm((D, RING * KV), BF),
             vm((RING, D, QW), BF),
@@ -460,7 +462,7 @@
         compiler_params=pltpu.CompilerParams(collective_id=1, has_side_effects=True, vmem_limit_bytes=62 * 2**20),
         cost_estimate=pl.CostEstimate(flops=13 * 10**9, bytes_accessed=20 * 2**20, transcendentals=2**22),
         name="attention_weight_gradient",
-    )(random_blocks, inputs[0], w_qkv, d_out[0])
+    )(random_blocks.T, inputs[0], w_qkv, d_out[0])
     attended, d_wqkv = pl.pallas_call(
         results_kernel,
         out_shape=[jax.ShapeDtypeStruct((TOK, D), BF), jax.ShapeDtypeStruct((16, RING * GW), F32)],

time: 95.6 us -> 93.8 us (0.981)
  local copies, waits for them, and re-layouts: 1.37 us -> 0 us
    unnamed x1 -> x0, local copies, waits for them, and re-layouts: 1.37 us -> none
where the time goes in v5:
time: 93.8 us; the launch traced here: 93.6 us
  Pallas kernels  93 us (99%)
    pallas_call x1, Pallas kernels, body(): pl.pallas_call(kernel, out_shape=[jax.ShapeDtypeStruct((RING, TOK, QW), B...  90.6 us
    pallas_call x1, Pallas kernels, body(): pl.pallas_call(results_kernel, out_shape=[jax.ShapeDtypeStruct((TOK, D),...  2.35 us

profile of v5, /device:TPU:1, one launch (start us, length us, event | category | flops | bytes accessed | tf_op | source)
XLA Modules:
  0.0 93.6 jit_solution(12452477966124493692)
XLA Ops:
  0.6 90.6 %attention_weight_gradient.1 = (bf16[4,256,512]{2,1,0:T(8,128)(2,1)}, bf16[2,4,16,768]{3,2,1,0:T(8,128)(2,1)}) custom-call(s32[3,32]{1,0:T(4,128)} %bitcast.7, bf16[256,2048]{1,0:T(8,128)(2,1)} %bitcast.4, bf16[2048,3072]{1,0:T(8,128)(2,1)} %w_ref.1, bf16[256,2048]{1,0:T(8,128)(2,1)} %bitcast.5), custom_call_target="tpu_custom_call" | custom-call | flops 12999999488 | bytes 20971520 | tf_op jit(solution)/shard_map/attention_weight_gradient/pallas_call | solution.py:418
  91.3 2.4 %results.1 = (bf16[256,2048]{1,0:T(8,128)(2,1)}, f32[16,3072]{1,0:T(8,128)}) custom-call(bf16[4,256,512]{2,1,0:T(8,128)(2,1)} %get-tuple-element.6.att_ref, bf16[2,4,16,768]{3,2,1,0:T(8,128)(2,1)} %get-tuple-element.7.sums_ref), custom_call_target="tpu_custom_call" | custom-call | tf_op jit(solution)/shard_map/results/pallas_call | solution.py:466
